TPU v7x, 512 devices: a whole 4x4x16 slice. The times are simulated.
512 devices in a mesh: corpus: 64 (over x, z), mp: 8 (over y, core).
Axes of the slice: x: 4, y: 4, z: 16, core: 2. Of those that a mesh axis runs over, the one named last changes fastest.
Arguments:
- question_word_vectors: bfloat16 [16, 32, 128], P('mp'), may hold values from -0.29882812 to 0.29882812
- document_word_vectors: bfloat16 [4096, 128, 128], P('corpus'), may hold values from -0.5 to 0.5
- document_extent: int32 [4096], P('corpus'), may hold values from 4 to 128
- shortlist_documents: int32 [16, 1024], P('mp'), may hold values from 0 to 4095, all different within a row
- retained_documents: int32 [16, 2], replicated, may hold values from 0 to 4095
- document_vocab_codes: int32 [4096, 32], P('corpus'), may hold values from 0 to 76799
- vocab_lookup_table: bfloat16 [76800, 4096], P('corpus', 'mp')
- prelayer_rms_gain: bfloat16 [4096], P('mp'), may hold values from 0.099609375 to 1.8984375
- gating_projector: bfloat16 [4096, 12288], P('mp', 'corpus'), may hold values from -0.09375 to 0.09375
- widening_projector: bfloat16 [4096, 12288], P('mp', 'corpus'), may hold values from -0.09375 to 0.09375
- reducing_projector: bfloat16 [12288, 4096], P('corpus', 'mp'), may hold values from -0.0546875 to 0.0546875
- merit_readout: float32 [4096], P('mp'), may hold values from -0.5 to 0.5
Outputs:
- shortlist_maxsim: float32 [16, 1024], replicated
- layer_result: bfloat16 [1024, 4096], P('corpus', 'mp')
- retained_merit: float32 [16, 2], replicated
Inputs may be any that keep to these rules, and one draw needn't show every extreme that they name: `shortlist_documents`: each row of candidates names 1024 different passages.
All inputs are finite; a program needn't handle non-finite values.
Results may differ from a plain program's by a relative error of at most 0.0034.
Values may be sent and summed in bfloat16 or wider, within the bound.
No kernel may reach another device: no remote copies, remote signals or barrier semaphores. Data moves between devices by JAX's collectives and lax.ppermute only.
A program may use at most 64 MiB of HBM per device.

v0:
```python
import jax
import jax.numpy as jnp
from jax import lax
from jax.sharding import PartitionSpec as P


def body(
    question_word_vectors,
    document_word_vectors,
    document_extent,
    shortlist_documents,
    retained_documents,
    document_vocab_codes,
    vocab_lookup_table,
    prelayer_rms_gain,
    gating_projector,
    widening_projector,
    reducing_projector,
    merit_readout,
):
    corpus_index = lax.axis_index("corpus")
    model_index = lax.axis_index("mp")
    query_count = question_word_vectors.shape[0]
    pass_count = document_word_vectors.shape[0]
    pass_slots = document_word_vectors.shape[1]
    vector_dim = document_word_vectors.shape[2]
    flat_queries = question_word_vectors.reshape(-1, vector_dim)
    flat_vectors = document_word_vectors.reshape(-1, vector_dim)
    dots = lax.dot_general(
        flat_queries, flat_vectors, (((1,), (1,)), ((), ())), preferred_element_type=jnp.float32
    )
    dots = dots.reshape(query_count, -1, pass_count, pass_slots)
    valid = jnp.arange(pass_slots, dtype=jnp.int32)[None, :] < document_extent[:, None]
    best = jnp.max(jnp.where(valid[None, None], dots, jnp.float32(-1e30)), axis=3)
    local_scores = jnp.sum(best, axis=1)
    pass_offset = corpus_index * pass_count
    local_ids = shortlist_documents - pass_offset
    owned = (local_ids >= 0) & (local_ids < pass_count)
    picked = jnp.take_along_axis(local_scores, jnp.clip(local_ids, 0, pass_count - 1), axis=1)
    picked = jnp.where(owned, picked, jnp.float32(0.0))
    all_queries = query_count * lax.axis_size("mp")
    cand_full = lax.dynamic_update_slice(
        jnp.zeros((all_queries, shortlist_documents.shape[1]), jnp.float32),
        picked,
        (model_index * query_count, jnp.int32(0)),
    )
    chosen_positions = retained_documents.reshape(-1)
    seq_count = chosen_positions.shape[0]
    seq_width = document_vocab_codes.shape[1]
    local_chosen = chosen_positions - pass_offset
    holds = (local_chosen >= 0) & (local_chosen < pass_count)
    safe_chosen = jnp.clip(local_chosen, 0, pass_count - 1)
    texts = jnp.where(holds[:, None], document_vocab_codes[safe_chosen], -1)
    lengths = jnp.where(holds, document_extent[safe_chosen], -1)
    texts, lengths = lax.pmax((texts, lengths), "corpus")
    seq_len = jnp.minimum(lengths, seq_width)
    token_ids = texts.reshape(-1)
    vocab_rows = vocab_lookup_table.shape[0]
    local_tokens = token_ids - corpus_index * vocab_rows
    in_range = (local_tokens >= 0) & (local_tokens < vocab_rows)
    looked = jnp.where(
        in_range[:, None],
        vocab_lookup_table[jnp.clip(local_tokens, 0, vocab_rows - 1)].astype(jnp.float32),
        jnp.float32(0.0),
    )
    embedded = lax.psum(looked, "corpus").astype(jnp.bfloat16)
    wide = embedded.astype(jnp.float32)
    squares = jnp.sum(wide * wide, axis=1)
    scaled = (wide * prelayer_rms_gain.astype(jnp.float32)).astype(jnp.bfloat16)
    gate_part = jnp.dot(scaled, gating_projector, preferred_element_type=jnp.float32)
    up_part = jnp.dot(scaled, widening_projector, preferred_element_type=jnp.float32)
    model_width = lax.axis_size("mp") * wide.shape[1]
    gate_sum, up_sum, square_sum = lax.psum((gate_part, up_part, squares), "mp")
    rscale = lax.rsqrt(square_sum / model_width + 1e-06)
    hidden = (jax.nn.silu(rscale[:, None] * gate_sum) * (rscale[:, None] * up_sum)).astype(
        jnp.bfloat16
    )
    token_total = hidden.shape[0]
    share = token_total // lax.axis_size("corpus")
    down_share = lax.psum_scatter(
        jnp.dot(hidden, reducing_projector, preferred_element_type=jnp.float32),
        "corpus",
        scatter_dimension=0,
        tiled=True,
    )
    row_start = corpus_index * share
    own_rows = lax.dynamic_slice_in_dim(wide, row_start, share, 0)
    total = own_rows + down_share
    layer_result = total.astype(jnp.bfloat16)
    per_token = jnp.sum(total * merit_readout[None, :], axis=1)
    global_rows = row_start + jnp.arange(share, dtype=jnp.int32)
    seq_of_row = global_rows // seq_width
    row_len = seq_len[seq_of_row]
    readout_product = jnp.where(
        global_rows % seq_width < row_len, per_token, jnp.float32(0.0)
    ) / row_len.astype(jnp.float32)
    member = seq_of_row[:, None] == jnp.arange(seq_count, dtype=jnp.int32)[None, :]
    score_part = jnp.sum(jnp.where(member, readout_product[:, None], jnp.float32(0.0)), axis=0)
    shortlist_size, aggregate_merit = lax.psum((cand_full, score_part), ("corpus", "mp"))
    return (shortlist_size, layer_result, aggregate_merit.reshape(retained_documents.shape))


def solution(mesh):
    placed = (
        P("mp", None, None),
        P("corpus", None, None),
        P("corpus"),
        P("mp", None),
        P(),
        P("corpus", None),
        P("corpus", "mp"),
        P("mp"),
        P("mp", "corpus"),
        P("mp", "corpus"),
        P("corpus", "mp"),
        P("mp"),
    )
    return jax.shard_map(
        body, mesh=mesh, in_specs=placed, out_specs=(P(), P("corpus", "mp"), P()), check_vma=False
    )
```

profile of v0, /device:TPU:1, one launch (start us, length us, event | category | flops | bytes accessed | tf_op | source)
XLA Modules:
  0.0 1487.2 jit_solution(17041921412212019672)
XLA Ops:
  8.0 0.0 copy-start
  8.0 0.0 all-reduce.8.cloned.1.call-start
  8.1 0.8 subtract_clamp_fusion.1
  8.9 0.7 compare_and_fusion.1
  9.6 0.1 copy.28
  9.7 0.1 min.38
  9.8 0.8 copy.29
  10.6 0.1 copy.27
  10.7 0.1 and.72
  10.8 0.6 gather_fusion
  11.3 1.4 gather_fusion.2
  12.7 0.1 broadcast_select_fusion
  12.8 231.3 %all-reduce = (s32[32,32]{1,0:T(8,128)S(1)}, s32[32]{0:T(128)S(1)}) all-reduce(s32[32,32]{1,0:T(8,128)S(1)} %broadcast_select_fusion, s32[32]{0:T(128)S(1)} %broadcast_select_fusion.1), channel_id=1, replica_groups=mesh['corpus'=64,'mp'=8] {'corpus'}, use_global_device_ids=true, to_apply=%region_3.4 | all-reduce | flops 1056 | bytes 8448 | tf_op jit(solution)/shard_map/pmax | solution.py:55
  244.1 0.1 min.41
  244.2 0.1 and.74
  244.3 5.4 gather_fusion.1
  249.8 1.6 convert_select_fusion
  251.4 0.0 copy-start.7
  251.4 0.0 copy-start.3
  251.4 0.0 copy-start.4
  251.4 242.4 %all-reduce.9 = bf16[1024,512]{1,0:T(8,128)(2,1)S(1)} all-reduce(f32[1024,512]{1,0:T(8,128)} %convert_select_fusion), channel_id=1, replica_groups=mesh['corpus'=64,'mp'=8] {'corpus'}, use_global_device_ids=true, to_apply=%region_4.5 | all-reduce | flops 524288 | bytes 3145728 | tf_op jit(solution)/shard_map/psum | solution.py:66
  493.7 0.0 copy-done.7
  493.8 0.0 copy-done.3
  493.8 1.4 fusion.4
  495.2 0.0 copy-done.4
  495.2 0.0 copy-start.8
  495.2 1.4 fusion.5
  496.6 0.0 all-reduce.8.cloned.1.call-update
  496.6 0.0 reduce-scatter.2.cloned.1.call-start
  496.7 0.3 multiply_reduce_fusion
  496.9 122.0 %psum.44 = f32[1024]{0:T(1024)S(1)} all-reduce(f32[1024]{0:T(1024)S(1)} %multiply_reduce_fusion), channel_id=1, replica_groups=mesh['corpus'=64,'mp'=8] {'mp'}, use_global_device_ids=true, to_apply=%region_6.7 | all-reduce | flops 1024 | bytes 8192 | tf_op jit(solution)/shard_map/psum | solution.py:73
  618.9 55.3 %all-reduce.8.cloned.1.call-done = (f32[1024,192]{0,1:T(8,128)}, f32[1024,192]{0,1:T(8,128)}) async-done(((f32[1024,192]{0,1:T(8,128)}, f32[1024,192]{0,1:T(8,128)}), (f32[1024,192]{0,1:T(8,128)}, f32[1024,192]{0,1:T(8,128)})) %all-reduce.8.cloned.1.call-update) | async-done | bytes 1572880 | tf_op jit(solution)/shard_map/psum | solution.py:73
  674.2 0.0 copy-done.8
  674.2 3.2 fusion.6
  677.4 0.0 copy-start.5
  677.4 0.0 copy-start.1
  677.4 0.0 copy-start.9
  677.4 0.0 reduce-scatter.2.cloned.1.call-update
  677.4 0.0 all-reduce.6.cloned.1.call-start
  677.5 0.6 copy-done.5
  678.1 0.0 copy-done.1
  678.2 0.1 iota_compare_fusion
  678.2 0.0 copy-done
  678.2 0.0 copy-done.9
  678.2 0.9 select_reduce_fusion
  679.2 0.1 reduce_sum.36
  679.3 17.6 %gather_fusion.4 = f32[2048]{0:T(1024)S(1)} fusion(f32[2,64]{1,0:T(2,128)S(1)} %reduce_sum.36, s32[2048]{0:T(1024)S(1)} %bitcast.28), kind=kCustom, calls=%fused_computation.4 | custom fusion | bytes 32768 | tf_op jit(solution)/shard_map/jit(take_along_axis)/gather | solution.py:39
  696.9 0.0 copy-start.6
  696.9 0.0 copy-start.2
  696.9 0.6 copy-done.2
  697.6 0.0 all-reduce.6.cloned.1.call-update
  697.6 1.6 convert_element_type.30
  699.2 0.7 gather_fusion.3
  699.9 663.1 %reduce-scatter.2.cloned.1.call-done = f32[16,512]{1,0:T(8,128)} async-done(((f32[1024,512]{1,0:T(8,128)}), f32[16,512]{1,0:T(8,128)}) %reduce-scatter.2.cloned.1.call-update) | async-done | bytes 32784 | tf_op jit(solution)/shard_map/reduce_scatter | solution.py:80
  1363.0 0.0 copy-done.6
  1363.0 1.5 multiply_reduce_fusion.1
  1364.6 0.1 select_reduce_fusion.1
  1364.6 0.1 reshape.213
  1364.7 112.9 %psum.47 = f32[16,2]{1,0:T(8,128)S(1)} all-reduce(f32[16,2]{1,0:T(8,128)S(1)} %reshape.213), channel_id=1, replica_groups=mesh['corpus'=64,'mp'=8] {'corpus','mp'}, use_global_device_ids=true, to_apply=%region_13.14 | all-reduce | flops 32 | bytes 256 | tf_op jit(solution)/shard_map/psum | solution.py:99
  1477.6 0.6 copy.30
  1478.3 0.0 all-reduce.6.cloned.1.call-done
  1478.3 1.5 copy.41
  (19 shorter events, 0.2 us)
Async XLA Ops:
  8.0 670.2 %copy-start = (bf16[64,128,128]{2,1,0:T(8,128)(2,1)S(1)}, bf16[64,128,128]{2,1,0:T(8,128)(2,1)}, u32[]{:S(2)}) copy-start(bf16[64,128,128]{2,1,0:T(8,128)(2,1)} %param.13) | copy-start | bytes 6291460
  8.0 666.2 %all-reduce.8.cloned.1.call-start = ((), (), s32[]{:S(2)}) async-start(), calls=%async_computation.3 | async-start | bytes 3145728 | tf_op jit(solution)/shard_map/psum | solution.py:73
  251.4 242.4 %copy-start.7 = (bf16[512]{0:T(512)(128)(2,1)S(1)}, bf16[512]{0:T(512)(128)(2,1)}, u32[]{:S(2)}) copy-start(bf16[512]{0:T(512)(128)(2,1)} %param.19) | copy-start | bytes 3076
  251.4 242.4 %copy-start.3 = (bf16[512,192]{0,1:T(8,128)(2,1)S(1)}, bf16[512,192]{0,1:T(8,128)(2,1)}, u32[]{:S(2)}) copy-start(bf16[512,192]{0,1:T(8,128)(2,1)} %param.21) | copy-start | bytes 589828
  251.4 243.8 %copy-start.4 = (bf16[512,192]{0,1:T(8,128)(2,1)S(1)}, bf16[512,192]{0,1:T(8,128)(2,1)}, u32[]{:S(2)}) copy-start(bf16[512,192]{0,1:T(8,128)(2,1)} %param.20) | copy-start | bytes 589828
  495.2 179.0 %copy-start.8 = (bf16[192,512]{1,0:T(8,128)(2,1)S(1)}, bf16[192,512]{1,0:T(8,128)(2,1)}, u32[]{:S(2)}) copy-start(bf16[192,512]{1,0:T(8,128)(2,1)} %param.22) | copy-start | bytes 589828
  496.6 866.4 %reduce-scatter.2.cloned.1.call-start = ((), (), s32[]{:S(2)}) async-start(), calls=%async_computation.2 | async-start | bytes 2129920 | tf_op jit(solution)/shard_map/reduce_scatter | solution.py:80
  677.4 0.7 copy-start.5
  677.4 0.7 copy-start.1
  677.4 0.8 copy-start.9
  677.4 800.8 %all-reduce.6.cloned.1.call-start = ((), (), s32[]{:S(2)}) async-start(), calls=%async_computation.1 | async-start | bytes 131072 | tf_op jit(solution)/shard_map/psum | solution.py:99
  696.9 666.2 %copy-start.6 = (f32[512]{0:T(512)S(1)}, f32[512]{0:T(512)}, u32[]{:S(2)}) copy-start(f32[512]{0:T(512)} %param.23) | copy-start | bytes 6148
  696.9 0.6 copy-start.2
Sparse Core Ops, SparseCore 0:
  496.7 177.4 all-reduce.7
  679.2 683.7 reduce-scatter.1
Sparse Core Ops, SparseCore 1:
  697.7 446.6 all-reduce.5
where the time goes:
time: 1490 us
  waiting for transfers between devices  718 us (48%)
  blocking collectives  709 us (48%)
  local copies, waits for them, and re-layouts  30.4 us (2%)
  between operations  15.7 us (1%)
    reduce_scatter x1, waiting for transfers between devices, body(): lax.psum_scatter(jnp.dot(hidden, reducing_projector, preferred_element_ty...  663 us
    psum x1, blocking collectives, body(): embedded = lax.psum(looked, 'corpus').astype(jnp.bfloat16)  242 us
    pmax x1, blocking collectives, body(): texts, lengths = lax.pmax((texts, lengths), 'corpus')  231 us
    psum x1, blocking collectives, body(): gate_sum, up_sum, square_sum = lax.psum((gate_part, up_part, squares), 'mp')  122 us
    psum x1, blocking collectives, body(): lax.psum((cand_full, score_part), ('corpus', 'mp'))  113 us
    psum x1, waiting for transfers between devices, body(): gate_sum, up_sum, square_sum = lax.psum((gate_part, up_part, squares), 'mp')  55.3 us
  transfers between devices with their start and end apart: 3, of which 2 were waited for; matrix products, arithmetic and copies ran while one was open for 2% of the time, Pallas kernels for 0%

commit v1 on v0

v1 whole, which is shorter than its diff:
```python
import jax
import jax.numpy as jnp
from jax import lax
from jax.sharding import Mesh, PartitionSpec as P

NX, NZ = 4, 16
F32, BF16 = jnp.float32, jnp.bfloat16


def split3(v):
    high = lax.reduce_precision(v, 8, 7)
    rest = v - high
    mid = lax.reduce_precision(rest, 8, 7)
    low = lax.reduce_precision(rest - mid, 8, 7)
    return jnp.stack([high, mid, low]).astype(BF16)


def join3(parts, axis=0):
    return jnp.sum(parts.astype(F32), axis=axis)


def swap(v, axis):
    return lax.all_to_all(v, axis, 0, 0, tiled=True)


def share(v, axis, n):
    return swap(jnp.broadcast_to(v[None], (n, *v.shape)), axis)


def rows_of(values, rows, columns):
    flat = values.reshape(-1)
    return jnp.pad(flat, (0, rows * columns - flat.shape[0])).reshape(rows, columns)


def body(
    question_word_vectors,
    document_word_vectors,
    document_extent,
    shortlist_documents,
    retained_documents,
    document_vocab_codes,
    vocab_lookup_table,
    prelayer_rms_gain,
    gating_projector,
    widening_projector,
    reducing_projector,
    merit_readout,
):
    n_mp = lax.axis_size("mp")
    corpus_index = lax.axis_index("x") * NZ + lax.axis_index("z")
    query_count = question_word_vectors.shape[0]
    pass_count, pass_slots, vector_dim = document_word_vectors.shape
    width = vocab_lookup_table.shape[1]
    hidden_units = gating_projector.shape[1]
    seq_count = retained_documents.size
    seq_width = document_vocab_codes.shape[1]
    tokens = seq_count * seq_width

    with jax.named_scope("token_ids"):
        pass_offset = corpus_index * pass_count
        chosen = retained_documents.reshape(-1) - pass_offset
        mine = chosen[:, None] == jnp.arange(pass_count, dtype=jnp.int32)[None, :]
        valid = jnp.arange(seq_width, dtype=jnp.int32)[None, :] < document_extent[:, None]
        coded = document_vocab_codes * 2 + valid.astype(jnp.int32)
        coded = jnp.sum(jnp.where(mine[:, :, None], coded[None], 0), axis=1)
        coded = coded.reshape(tokens // 128, 128)
        coded = jnp.sum(share(coded, "z", NZ), axis=0)
        coded = jnp.sum(share(coded, "x", NX), axis=0)
        coded = coded.reshape(tokens)
        token_ids = coded // 2
        token_valid = (coded % 2).reshape(seq_count, seq_width)
        weight = token_valid.astype(F32) / jnp.sum(token_valid, axis=1, keepdims=True).astype(F32)

    with jax.named_scope("passage_scores"):
        dots = lax.dot_general(
            question_word_vectors.reshape(-1, vector_dim),
            document_word_vectors.reshape(-1, vector_dim),
            (((1,), (1,)), ((), ())),
            preferred_element_type=F32,
        ).reshape(query_count, -1, pass_count, pass_slots)
        slots = jnp.arange(pass_slots, dtype=jnp.int32)[None, :] < document_extent[:, None]
        best = jnp.max(jnp.where(slots[None, None], dots, F32(-1e30)), axis=3)
        scores = jnp.sum(best, axis=1)

    with jax.named_scope("embedded"):
        vocab_rows = vocab_lookup_table.shape[0]
        local_ids = token_ids - corpus_index * vocab_rows
        chosen_rows = (
            local_ids[:, None] == jnp.arange(vocab_rows, dtype=jnp.int32)[None, :]
        ).astype(BF16)
        looked = jnp.dot(chosen_rows, vocab_lookup_table, preferred_element_type=F32).astype(BF16)
        looked = swap(looked.reshape(NX, tokens // NX, width), "x")
        looked = jnp.sum(looked.astype(F32), axis=0).astype(BF16)
        looked = swap(looked.reshape(NZ, -1, width), "z")
        own_rows = jnp.sum(looked.astype(F32), axis=0)
        share_rows = own_rows.shape[0]
        score_rows = rows_of(split3(scores), 8, width)
        block = jnp.concatenate([own_rows.astype(BF16), score_rows], axis=0)
        block = share(block, "z", NZ).reshape(-1, width)
        block = share(block, "x", NX).reshape(NX * NZ, share_rows + 8, width)
        embedded = block[:, :share_rows].reshape(tokens, width)
        all_scores = block[:, share_rows:].reshape(NX * NZ, -1)[:, : 3 * scores.size]
        all_scores = join3(all_scores.reshape(NX * NZ, 3, query_count, pass_count), axis=1)
        all_scores = jnp.transpose(all_scores, (1, 0, 2)).reshape(query_count, -1)

    with jax.named_scope("shortlist"):
        high, low = shortlist_documents // 128, shortlist_documents % 128
        at_high = (high[:, :, None] == jnp.arange(all_scores.shape[1] // 128)[None, None]).astype(F32)
        table = all_scores.reshape(query_count, -1, 128)
        lines = lax.dot_general(
            at_high, table, (((2,), (1,)), ((0,), (0,))), precision=lax.Precision.HIGHEST
        )
        at_low = low[:, :, None] == jnp.arange(128)[None, None]
        picked = jnp.sum(jnp.where(at_low, lines, F32(0.0)), axis=2)

    with jax.named_scope("gate_up"):
        wide = embedded.astype(F32)
        squares = jnp.sum(wide * wide, axis=1)
        readings = jnp.sum(wide * merit_readout[None, :], axis=1)
        scaled = (wide * prelayer_rms_gain.astype(F32)).astype(BF16)
        both = jnp.concatenate([gating_projector, widening_projector], axis=1)
        part = jnp.dot(scaled, both, preferred_element_type=F32).astype(BF16)
        part = part.reshape(n_mp, tokens // n_mp, 2 * hidden_units)
        sums = jnp.stack([squares.reshape(n_mp, -1), readings.reshape(n_mp, -1)], axis=1)
        sums = jnp.moveaxis(split3(sums), 0, 1).reshape(n_mp, -1)
        sums = jnp.pad(sums, ((0, 0), (0, 16 * hidden_units - sums.shape[1])))
        part = jnp.concatenate([part, sums.reshape(n_mp, 8, 2 * hidden_units)], axis=1)
        part = swap(part, "mp")
        total_part = jnp.sum(part[:, : tokens // n_mp].astype(F32), axis=0)
        sums = part[:, tokens // n_mp :].reshape(n_mp, -1)[:, : 6 * (tokens // n_mp)]
        sums = jnp.sum(sums.astype(F32).reshape(n_mp * 3, 2, tokens // n_mp), axis=0)
        rscale = lax.rsqrt(sums[0] / (n_mp * width) + 1e-06)[:, None]
        gate, up = total_part[:, :hidden_units], total_part[:, hidden_units:]
        hidden = (jax.nn.silu(rscale * gate) * (rscale * up)).astype(BF16)

    with jax.named_scope("hidden"):
        extra = jnp.concatenate([split3(sums[1]).reshape(-1), split3(picked).reshape(-1)])
        extra_rows = -(-extra.size // (hidden_units * 16)) * 16
        block = jnp.concatenate([hidden, rows_of(extra, extra_rows, hidden_units)], axis=0)
        block = share(block, "mp", n_mp)
        hidden = block[:, : tokens // n_mp].reshape(tokens, hidden_units)
        extra = block[:, tokens // n_mp :].reshape(n_mp, -1)
        cut = 3 * tokens // n_mp
        readings = join3(extra[:, :cut].reshape(n_mp, 3, -1), axis=1).reshape(tokens)
        shortlist_maxsim = join3(
            extra[:, cut : cut + 3 * picked.size].reshape(n_mp, 3, *picked.shape), axis=1
        ).reshape(-1, picked.shape[1])

    with jax.named_scope("down"):
        line = lax.psum(
            jnp.sum(reducing_projector.astype(F32) * merit_readout[None, :], axis=1), "mp"
        )
        merit = jnp.sum(hidden.astype(F32) * line[None, :], axis=1)
        merit = jnp.sum(merit.reshape(seq_count, seq_width) * weight, axis=1)
        down = jnp.dot(hidden, reducing_projector, preferred_element_type=F32).astype(BF16)
        down = down.reshape(NX, tokens // NX, width)
        rider = rows_of(split3(merit), 8, width)
        down = jnp.concatenate([down, jnp.broadcast_to(rider[None], (NX, 8, width))], axis=1)
        down = swap(down, "x")
        rider = down[:, tokens // NX :].reshape(NX, -1)[:, : 3 * seq_count]
        merit = jnp.sum(rider.reshape(NX * 3, seq_count).astype(F32), axis=0)
        down = jnp.sum(down[:, : tokens // NX].astype(F32), axis=0).astype(BF16)
        down = down.reshape(NZ, -1, width)
        rider = rows_of(split3(merit), 8, width)
        down = jnp.concatenate([down, jnp.broadcast_to(rider[None], (NZ, 8, width))], axis=1)
        down = swap(down, "z")
        rider = down[:, share_rows:].reshape(NZ, -1)[:, : 3 * seq_count]
        merit = jnp.sum(rider.reshape(NZ * 3, seq_count).astype(F32), axis=0)
        total = own_rows + jnp.sum(down[:, :share_rows].astype(F32), axis=0)
        layer_result = total.astype(BF16)
        merit = merit + jnp.sum(readings.reshape(seq_count, seq_width) * weight, axis=1)

    return (shortlist_maxsim, layer_result, merit.reshape(retained_documents.shape))


def solution(mesh):
    split = Mesh(mesh.devices.reshape(NX, NZ, -1), ("x", "z", "mp"))
    corpus = ("x", "z")
    placed = (
        P("mp", None, None),
        P(corpus, None, None),
        P(corpus),
        P("mp", None),
        P(),
        P(corpus, None),
        P(corpus, "mp"),
        P("mp"),
        P("mp", corpus),
        P("mp", corpus),
        P(corpus, "mp"),
        P("mp"),
    )
    return jax.shard_map(
        body, mesh=split, in_specs=placed, out_specs=(P(), P(corpus, "mp"), P()), check_vma=False
    )
```

time: 1490 us -> 236 us (0.16)
  the two profiles are of different devices: /device:TPU:1 before, /device:TPU:16 now
where the time goes in v1:
time: 236 us; the launch traced here: 235 us
  blocking collectives  103 us (44%)
  waiting for transfers between devices  62.7 us (27%)
  starting transfers between devices  36.4 us (15%)
  other arithmetic  15.7 us (7%)
  local copies, waits for them, and re-layouts  10.2 us (4%)
  matrix products  5.65 us (2%)
    all_to_all x4, blocking collectives, swap(): return lax.all_to_all(v, axis, 0, 0, tiled=True)  87.2 us
    all_to_all x6, waiting for transfers between devices, swap(): return lax.all_to_all(v, axis, 0, 0, tiled=True)  62.7 us
    all_to_all x6, starting transfers between devices, swap(): return lax.all_to_all(v, axis, 0, 0, tiled=True)  36.4 us
    psum x1, blocking collectives, body(): lax.psum(jnp.sum(reducing_projector.astype(F32) * merit_readout[None, :],...  15.6 us
  transfers between devices with their start and end apart: 6, of which 5 were waited for; matrix products, arithmetic and copies ran while one was open for 3% of the time, Pallas kernels for 0%

profile of v1, /device:TPU:16, one launch (start us, length us, event | category | flops | bytes accessed | tf_op | source)
XLA Modules:
  0.0 234.6 jit_solution(5375173241274152710)
XLA Ops:
  0.7 0.8 broadcast_subtract_fusion
  1.5 0.1 copy.39
  1.6 0.1 sub.166
  1.7 0.7 convert_add_fusion
  2.5 0.6 select_reduce_fusion.1
  3.2 27.7 %all_to_all.50 = s32[16,8,128]{2,1,0:T(8,128)S(1)} all-to-all(s32[16,8,128]{2,1,0:T(8,128)S(1)} %broadcast_in_dim.62), channel_id=1, replica_groups=mesh['x'=4,'z'=16,'mp'=8] {'z'}, dimensions={0} | all-to-all | bytes 131072 | tf_op jit(solution)/shard_map/token_ids/all_to_all | solution.py:23
  30.9 0.6 broadcast_in_dim.63
  31.5 4.3 %all-to-all-start.1 = ((s32[4,8,128]{2,1,0:T(8,128)}), s32[4,8,128]{2,1,0:T(8,128)S(1)}, u32[]{:S(2)}, u32[]{:S(2)}) async-start(s32[4,8,128]{2,1,0:T(8,128)} %broadcast_in_dim.63), calls=%async_computation.1 | async-start | bytes 32768 | tf_op jit(solution)/shard_map/token_ids/all_to_all | solution.py:23
  35.8 5.4 %all-to-all-done.1 = s32[4,8,128]{2,1,0:T(8,128)S(1)} async-done(((s32[4,8,128]{2,1,0:T(8,128)}), s32[4,8,128]{2,1,0:T(8,128)S(1)}, u32[]{:S(2)}, u32[]{:S(2)}) %all-to-all-start.1) | async-done | bytes 16416 | tf_op jit(solution)/shard_map/token_ids/all_to_all | solution.py:23
  41.2 2.9 %fusion.7 = bf16[1024,512]{1,0:T(8,128)(2,1)S(1)} fusion(bf16[1200,512]{1,0:T(8,128)(2,1)} %param.18, s32[1024]{0:T(1024)S(1)} %fusion.26), kind=kOutput, calls=%fused_computation.11 | convolution fusion | flops 1260044288 | bytes 2281472 | tf_op jit(solution)/shard_map/embedded/dot_general | solution.py:91
  44.1 14.9 %all_to_all.51 = bf16[4,256,512]{2,1,0:T(8,128)(2,1)S(1)} all-to-all(bf16[4,256,512]{2,1,0:T(8,128)(2,1)S(1)} %bitcast.110), channel_id=1, replica_groups=mesh['x'=4,'z'=16,'mp'=8] {'x'}, dimensions={0} | all-to-all | bytes 2097152 | tf_op jit(solution)/shard_map/embedded/all_to_all | solution.py:23
  59.0 0.9 reduce_sum.224
  59.9 3.5 %all-to-all-start.3 = ((bf16[16,16,512]{2,1,0:T(8,128)(2,1)}), bf16[16,16,512]{2,1,0:T(8,128)(2,1)S(1)}, u32[]{:S(2)}, u32[]{:S(2)}) async-start(bf16[16,16,512]{2,1,0:T(8,128)(2,1)} %bitcast.2), calls=%async_computation.3 | async-start | bytes 524288 | tf_op jit(solution)/shard_map/embedded/all_to_all | solution.py:23
  63.6 0.9 select_reduce_fusion
  64.5 0.1 reduce_sum.226
  64.6 0.1 convert_element_type.140
  64.7 13.8 %all-to-all-done.3 = bf16[16,16,512]{2,1,0:T(8,128)(2,1)S(1)} async-done(((bf16[16,16,512]{2,1,0:T(8,128)(2,1)}), bf16[16,16,512]{2,1,0:T(8,128)(2,1)S(1)}, u32[]{:S(2)}, u32[]{:S(2)}) %all-to-all-start.3) | async-done | bytes 262176 | tf_op jit(solution)/shard_map/embedded/all_to_all | solution.py:23
  78.7 0.6 copy-done.3
  79.3 26.3 %all_to_all.52 = bf16[16,24,512]{2,1,0:T(8,128)(2,1)S(1)} all-to-all(bf16[16,24,512]{2,1,0:T(8,128)(2,1)S(1)} %broadcast_in_dim.66), channel_id=1, replica_groups=mesh['x'=4,'z'=16,'mp'=8] {'z'}, dimensions={0} | all-to-all | bytes 786432 | tf_op jit(solution)/shard_map/embedded/all_to_all | solution.py:23
  105.6 1.3 broadcast_in_dim.68
  106.9 4.4 %all-to-all-start.5 = ((bf16[4,384,512]{2,1,0:T(8,128)(2,1)}), bf16[4,384,512]{2,1,0:T(8,128)(2,1)}, u32[]{:S(2)}, u32[]{:S(2)}) async-start(bf16[4,384,512]{2,1,0:T(8,128)(2,1)} %broadcast_in_dim.68), calls=%async_computation.5 | async-start | bytes 3145728 | tf_op jit(solution)/shard_map/embedded/all_to_all | solution.py:23
  111.3 13.7 %all-to-all-done.5 = bf16[4,384,512]{2,1,0:T(8,128)(2,1)} async-done(((bf16[4,384,512]{2,1,0:T(8,128)(2,1)}), bf16[4,384,512]{2,1,0:T(8,128)(2,1)}, u32[]{:S(2)}, u32[]{:S(2)}) %all-to-all-start.5) | async-done | bytes 1572896 | tf_op jit(solution)/shard_map/embedded/all_to_all | solution.py:23
  125.0 2.9 %slice_convert_fusion = f32[64,16,512]{2,1,0:T(8,128)} fusion(bf16[64,24,512]{2,1,0:T(8,128)(2,1)} %bitcast.8), kind=kLoop, calls=%fused_computation.18 | loop fusion | flops 524288 | bytes 3145728 | tf_op jit(solution)/shard_map/gate_up/convert_element_type | solution.py:117
  127.9 1.7 multiply_reduce_fusion
  129.6 0.1 stack.50
  129.8 1.9 fusion.2
  131.7 0.7 convolution_convert_fusion.1
  132.4 1.0 pad_maximum_fusion.1
  133.4 4.8 %all-to-all-start.6 = ((bf16[8,136,384]{2,1,0:T(8,128)(2,1)}), bf16[8,136,384]{2,1,0:T(8,128)(2,1)S(1)}, u32[]{:S(2)}, u32[]{:S(2)}) async-start(bf16[8,136,384]{2,1,0:T(8,128)(2,1)} %pad_maximum_fusion.1), calls=%async_computation.6 | async-start | bytes 1671168 | tf_op jit(solution)/shard_map/gate_up/all_to_all | solution.py:23
  138.3 1.1 slice.86
  139.4 0.2 copy.52
  139.6 0.2 reshape.494
  139.7 0.1 reduce_sum.232
  140.0 0.7 fusion.8
  140.7 8.0 %all-to-all-done.6 = bf16[8,136,384]{2,1,0:T(8,128)(2,1)S(1)} async-done(((bf16[8,136,384]{2,1,0:T(8,128)(2,1)}), bf16[8,136,384]{2,1,0:T(8,128)(2,1)S(1)}, u32[]{:S(2)}, u32[]{:S(2)}) %all-to-all-start.6) | async-done | bytes 835616 | tf_op jit(solution)/shard_map/gate_up/all_to_all | solution.py:23
  148.9 0.1 reshape.480
  149.0 0.1 convert_reduce_fusion
  149.1 0.1 fusion.13
  149.3 0.9 broadcast_in_dim.115
  150.2 6.6 %all-to-all-start.7 = ((bf16[8,176,192]{2,1,0:T(8,128)(2,1)}), bf16[8,176,192]{2,1,0:T(8,128)(2,1)S(1)}, u32[]{:S(2)}, u32[]{:S(2)}) async-start(bf16[8,176,192]{2,1,0:T(8,128)(2,1)} %broadcast_in_dim.115), calls=%async_computation.7 | async-start | bytes 1441792 | tf_op jit(solution)/shard_map/hidden/all_to_all | solution.py:23
  156.8 0.1 multiply_reduce_fusion.3
  156.9 15.6 %psum.7 = f32[192]{0:T(256)} all-reduce(f32[192]{0:T(256)S(1)} %multiply_reduce_fusion.3), channel_id=1, replica_groups=mesh['x'=4,'z'=16,'mp'=8] {'mp'}, use_global_device_ids=true, to_apply=%region_15.16 | all-reduce | flops 192 | bytes 1536 | tf_op jit(solution)/shard_map/down/psum | solution.py:150
  172.5 0.8 reshape.486
  173.2 0.1 fusion.24
  173.3 0.5 convert_element_type.159
  173.9 0.2 reshape.481
  174.1 0.6 copy-done.2
  174.7 0.7 reshape.490
  175.5 0.3 copy.47
  175.7 0.8 multiply_reduce_fusion.2
  176.6 0.9 multiply_reduce_fusion.4
  177.6 0.1 convert_element_type.160
  177.7 0.4 convolution_convert_fusion
  178.1 0.1 pad_maximum_fusion
  178.2 18.3 %all_to_all.53 = bf16[4,264,512]{2,1,0:T(8,128)(2,1)S(1)} all-to-all(bf16[4,264,512]{2,1,0:T(8,128)(2,1)S(1)} %pad_maximum_fusion), channel_id=1, replica_groups=mesh['x'=4,'z'=16,'mp'=8] {'x'}, dimensions={0} | all-to-all | bytes 2162688 | tf_op jit(solution)/shard_map/down/all_to_all | solution.py:23
  196.7 0.1 convert_element_type.163
  196.8 0.1 slice_reduce_fusion
  196.9 0.8 pad_maximum_fusion.2
  197.7 12.8 %all-to-all-start.9 = ((bf16[16,24,512]{2,1,0:T(8,128)(2,1)}), bf16[16,24,512]{2,1,0:T(8,128)(2,1)S(1)}, u32[]{:S(2)}, u32[]{:S(2)}) async-start(bf16[16,24,512]{2,1,0:T(8,128)(2,1)} %pad_maximum_fusion.2), calls=%async_computation.9 | async-start | bytes 786432 | tf_op jit(solution)/shard_map/down/all_to_all | solution.py:23
  210.6 0.7 reshape.482
  211.3 21.7 %all-to-all-done.9 = bf16[16,24,512]{2,1,0:T(8,128)(2,1)S(1)} async-done(((bf16[16,24,512]{2,1,0:T(8,128)(2,1)}), bf16[16,24,512]{2,1,0:T(8,128)(2,1)S(1)}, u32[]{:S(2)}, u32[]{:S(2)}) %all-to-all-start.9) | async-done | bytes 393248 | tf_op jit(solution)/shard_map/down/all_to_all | solution.py:23
  233.1 0.6 add_convert_fusion
  233.8 0.1 add.71
  233.9 0.7 copy.44
  (94 shorter events, 1.5 us)
Async XLA Ops:
  0.6 62.9 %copy-start = (bf16[64,128,128]{2,1,0:T(8,128)(2,1)S(1)}, bf16[64,128,128]{2,1,0:T(8,128)(2,1)}, u32[]{:S(2)}) copy-start(bf16[64,128,128]{2,1,0:T(8,128)(2,1)} %param.13) | copy-start | bytes 6291460
  31.5 9.7 %all-to-all-start.1 = ((s32[4,8,128]{2,1,0:T(8,128)}), s32[4,8,128]{2,1,0:T(8,128)S(1)}, u32[]{:S(2)}, u32[]{:S(2)}) async-start(s32[4,8,128]{2,1,0:T(8,128)} %broadcast_in_dim.63), calls=%async_computation.1 | async-start | bytes 32768 | tf_op jit(solution)/shard_map/token_ids/all_to_all | solution.py:23
  41.2 2.9 %copy-start.5 = (s32[8,128]{1,0:T(8,128)}, s32[8,128]{1,0:T(8,128)S(1)}, u32[]{:S(2)}) copy-start(s32[8,128]{1,0:T(8,128)S(1)} %reduce_sum.223) | copy-start | bytes 12292
  44.1 19.4 %copy-start.8 = (s32[64]{0:T(128)S(1)}, s32[64]{0:T(128)}, u32[]{:S(2)}) copy-start(s32[64]{0:T(128)} %param.14) | copy-start | bytes 772
  44.1 19.5 %copy-start.12 = (bf16[2,32,128]{2,1,0:T(8,128)(2,1)S(1)}, bf16[2,32,128]{2,1,0:T(8,128)(2,1)}, u32[]{:S(2)}) copy-start(bf16[2,32,128]{2,1,0:T(8,128)(2,1)} %param.12) | copy-start | bytes 49156
  59.9 18.7 %all-to-all-start.3 = ((bf16[16,16,512]{2,1,0:T(8,128)(2,1)}), bf16[16,16,512]{2,1,0:T(8,128)(2,1)S(1)}, u32[]{:S(2)}, u32[]{:S(2)}) async-start(bf16[16,16,512]{2,1,0:T(8,128)(2,1)} %bitcast.2), calls=%async_computation.3 | async-start | bytes 524288 | tf_op jit(solution)/shard_map/embedded/all_to_all | solution.py:23
  78.6 0.6 copy-start.3
  105.6 5.6 %copy-start.9 = (bf16[512]{0:T(512)(128)(2,1)S(1)}, bf16[512]{0:T(512)(128)(2,1)}, u32[]{:S(2)}) copy-start(bf16[512]{0:T(512)(128)(2,1)} %param.19) | copy-start | bytes 3076
  106.9 18.1 %all-to-all-start.5 = ((bf16[4,384,512]{2,1,0:T(8,128)(2,1)}), bf16[4,384,512]{2,1,0:T(8,128)(2,1)}, u32[]{:S(2)}, u32[]{:S(2)}) async-start(bf16[4,384,512]{2,1,0:T(8,128)(2,1)} %broadcast_in_dim.68), calls=%async_computation.5 | async-start | bytes 3145728 | tf_op jit(solution)/shard_map/embedded/all_to_all | solution.py:23
  111.2 16.6 %copy-start.6 = (f32[512]{0:T(512)S(1)}, f32[512]{0:T(512)}, u32[]{:S(2)}) copy-start(f32[512]{0:T(512)} %param.23) | copy-start | bytes 6148
  127.9 3.8 %copy-start.10 = (bf16[512,192]{0,1:T(8,128)(2,1)S(1)}, bf16[512,192]{0,1:T(8,128)(2,1)}, u32[]{:S(2)}) copy-start(bf16[512,192]{0,1:T(8,128)(2,1)} %param.21) | copy-start | bytes 589828
  127.9 3.8 %copy-start.11 = (bf16[512,192]{0,1:T(8,128)(2,1)S(1)}, bf16[512,192]{0,1:T(8,128)(2,1)}, u32[]{:S(2)}) copy-start(bf16[512,192]{0,1:T(8,128)(2,1)} %param.20) | copy-start | bytes 589828
  132.4 5.8 %copy-start.7 = (s32[2,1024]{1,0:T(2,128)S(1)}, s32[2,1024]{1,0:T(2,128)}, u32[]{:S(2)}) copy-start(s32[2,1024]{1,0:T(2,128)} %param.15) | copy-start | bytes 24580
  133.4 15.3 %all-to-all-start.6 = ((bf16[8,136,384]{2,1,0:T(8,128)(2,1)}), bf16[8,136,384]{2,1,0:T(8,128)(2,1)S(1)}, u32[]{:S(2)}, u32[]{:S(2)}) async-start(bf16[8,136,384]{2,1,0:T(8,128)(2,1)} %pad_maximum_fusion.1), calls=%async_computation.6 | async-start | bytes 1671168 | tf_op jit(solution)/shard_map/gate_up/all_to_all | solution.py:23
  140.7 16.1 %copy-start.1 = (bf16[192,512]{1,0:T(8,128)(2,1)S(1)}, bf16[192,512]{1,0:T(8,128)(2,1)}, u32[]{:S(2)}) copy-start(bf16[192,512]{1,0:T(8,128)(2,1)} %param.22) | copy-start | bytes 589828
  150.2 23.7 %all-to-all-start.7 = ((bf16[8,176,192]{2,1,0:T(8,128)(2,1)}), bf16[8,176,192]{2,1,0:T(8,128)(2,1)S(1)}, u32[]{:S(2)}, u32[]{:S(2)}) async-start(bf16[8,176,192]{2,1,0:T(8,128)(2,1)} %broadcast_in_dim.115), calls=%async_computation.7 | async-start | bytes 1441792 | tf_op jit(solution)/shard_map/hidden/all_to_all | solution.py:23
  174.1 0.7 copy-start.2
  196.5 14.0 %slice-start = ((bf16[8,9216]{1,0:T(8,128)(2,1)}), bf16[8,6144]{1,0:T(8,128)(2,1)S(1)}, s32[]{:S(2)}) async-start(bf16[8,9216]{1,0:T(8,128)(2,1)} %copy-done.2), calls=%async_computation.10 | async-start | bytes 196608 | tf_op jit(solution)/shard_map/hidden/slice | solution.py:146
  196.5 36.6 %copy-start.4 = (f32[16,512]{1,0:T(8,128)S(1)}, f32[16,512]{1,0:T(8,128)}, u32[]{:S(2)}) copy-start(f32[16,512]{1,0:T(8,128)} %copy-done.3) | copy-start | bytes 98308
  197.7 35.3 %all-to-all-start.9 = ((bf16[16,24,512]{2,1,0:T(8,128)(2,1)}), bf16[16,24,512]{2,1,0:T(8,128)(2,1)S(1)}, u32[]{:S(2)}, u32[]{:S(2)}) async-start(bf16[16,24,512]{2,1,0:T(8,128)(2,1)} %pad_maximum_fusion.2), calls=%async_computation.9 | async-start | bytes 786432 | tf_op jit(solution)/shard_map/down/all_to_all | solution.py:23

commit v2 on v1

v2 whole, which is shorter than its diff:
```python
import functools

import jax
import jax.numpy as jnp
from jax import lax
from jax.experimental import pallas as pl
from jax.experimental.pallas import tpu as pltpu
from jax.sharding import Mesh, PartitionSpec as P

NX, NZ = 4, 16
LANES = 128
F32, BF16 = jnp.float32, jnp.bfloat16
CORPUS = ("x", "z")
TRANSPOSED = (((1,), (1,)), ((), ()))


def split3(v):
    high = lax.reduce_precision(v, 8, 7)
    rest = v - high
    mid = lax.reduce_precision(rest, 8, 7)
    low = lax.reduce_precision(rest - mid, 8, 7)
    return jnp.stack([high, mid, low]).astype(BF16)


def swap(v, axis):
    return lax.all_to_all(v, axis, 0, 0, tiled=True)


def share_with(v, axis, n):
    return swap(jnp.broadcast_to(v[None], (n, *v.shape)), axis)


def terms(v):
    high = v.astype(BF16).astype(F32)
    mid = (v - high).astype(BF16).astype(F32)
    return high, mid, v - high - mid


def fill(shape, axis, pieces):
    place = lax.broadcasted_iota(jnp.int32, shape, axis)
    block = jnp.zeros(shape, F32)
    for i, piece in enumerate(pieces):
        block = jnp.where(place == i, piece, block)
    return block


def gate_up_kernel(
    n_mp, units, rows_ref, gain_ref, readout_ref, w0_ref, w1_ref, w2_ref, w3_ref, out_ref, first, second
):
    parts = (w0_ref, w1_ref, w2_ref, w3_ref)
    half = NX * units
    for i, part in enumerate(parts):
        first[i * units : (i + 1) * units, :] = part[:units, :]
        first[half + i * units : half + (i + 1) * units, :] = part[units : 2 * units, :]
        second[i * units : (i + 1) * units, :] = part[2 * units :, :]
    value = rows_ref[...].astype(F32)
    squares = jnp.sum(value * value, axis=1, keepdims=True)
    reading = jnp.sum(value * readout_ref[...], axis=1, keepdims=True)
    scaled = (value * gain_ref[...]).astype(BF16)
    both = lax.dot_general(scaled, first[...], TRANSPOSED, preferred_element_type=F32)
    per_token = fill((value.shape[0], LANES), 1, (*terms(squares), *terms(reading)))

    readout = fill((16, value.shape[1]), 0, terms(readout_ref[...])).astype(BF16)
    line = lax.dot_general(readout, second[...], TRANSPOSED, preferred_element_type=F32)
    line = jnp.sum(line, axis=0, keepdims=True)
    pieces = [
        term[:, at : at + LANES] for term in terms(line) for at in range(0, half, LANES)
    ]
    share = value.shape[0] // n_mp
    line = fill((share, LANES), 0, pieces).astype(BF16)
    for target in range(n_mp):
        take = slice(target * share, (target + 1) * share)
        out_ref[target, :, : 2 * half] = both[take].astype(BF16)
        out_ref[target, :, 2 * half : 2 * half + LANES] = per_token[take].astype(BF16)
        out_ref[target, :, 2 * half + LANES :] = line


def hidden_kernel(n_mp, features, half, got_ref, weight_ref, picks_ref, out_ref):
    total = got_ref[0].astype(F32)
    for source in range(1, n_mp):
        total += got_ref[source].astype(F32)
    per_token = total[:, 2 * half : 2 * half + LANES]
    lane = lax.broadcasted_iota(jnp.int32, per_token.shape, 1)
    squares = jnp.sum(jnp.where(lane < 3, per_token, 0.0), axis=1, keepdims=True)
    reading = jnp.sum(jnp.where((lane >= 3) & (lane < 6), per_token, 0.0), axis=1, keepdims=True)
    rscale = lax.rsqrt(squares / features + 1e-06)
    gate, up = rscale * total[:, :half], rscale * total[:, half : 2 * half]
    hidden = (gate / (1.0 + jnp.exp(-gate)) * up).astype(BF16)
    line = total[:, 2 * half + LANES :]
    count = half // LANES
    merit = reading * (1.0 / NZ)
    for i in range(count):
        piece = line[i : i + 1] + line[count + i : count + i + 1] + line[2 * count + i : 2 * count + i + 1]
        merit += jnp.sum(
            hidden[:, i * LANES : (i + 1) * LANES].astype(F32) * piece, axis=1, keepdims=True
        )
    merit = jnp.sum(merit * weight_ref[:, :1], axis=0, keepdims=True)
    place = lax.broadcasted_iota(jnp.int32, per_token.shape, 0)
    rider = picks_ref[:, LANES:].astype(F32)
    for i, term in enumerate(terms(merit)):
        rider = jnp.where(place == 16 + i, term, rider)
    out_ref[:, :half] = hidden
    out_ref[:, half : half + LANES] = picks_ref[:, :LANES]
    out_ref[:, half + LANES :] = rider.astype(BF16)


def down_kernel(n_mp, units, half, got_ref, w0_ref, w1_ref, w2_ref, w3_ref, out_ref, second):
    for i, part in enumerate((w0_ref, w1_ref, w2_ref, w3_ref)):
        second[i * units : (i + 1) * units, :] = part[2 * units :, :]
    tokens = got_ref.shape[0] * got_ref.shape[1]
    hidden = got_ref[:, :, :half].reshape(tokens, half)
    down = jnp.dot(hidden, second[...], preferred_element_type=F32)
    groups = out_ref.shape[0]
    share = tokens // groups
    shares = got_ref[:, 16:, half + LANES :].astype(F32)
    rider = fill((n_mp, LANES), 1, (shares[:, 0], shares[:, 1], shares[:, 2]))
    rider = jnp.concatenate([rider, jnp.zeros((share - n_mp, LANES), F32)], axis=0).astype(BF16)
    for target in range(groups):
        out_ref[target, :, : down.shape[1]] = down[target * share : (target + 1) * share].astype(BF16)
        out_ref[target, :, down.shape[1] :] = rider


def body(
    question_word_vectors,
    document_word_vectors,
    document_extent,
    shortlist_documents,
    retained_documents,
    document_vocab_codes,
    vocab_lookup_table,
    prelayer_rms_gain,
    gating_projector,
    widening_projector,
    reducing_projector,
    merit_readout,
):
    n_mp = lax.axis_size("mp")
    x_index, z_index, mp_index = (lax.axis_index(name) for name in ("x", "z", "mp"))
    corpus_index = x_index * NZ + z_index
    query_count = question_word_vectors.shape[0]
    pass_count, pass_slots, vector_dim = document_word_vectors.shape
    vocab_rows, width = vocab_lookup_table.shape
    units = gating_projector.shape[1]
    half = NX * units
    seq_count = retained_documents.size
    seq_width = document_vocab_codes.shape[1]
    tokens = seq_count * seq_width
    share = tokens // (NX * NZ)
    own_tokens = tokens // NX // n_mp

    with jax.named_scope("weights"):
        weights = [jnp.concatenate([gating_projector.T, widening_projector.T, reducing_projector], axis=0)]
        pairs = [(i, (i + 1) % NX) for i in range(NX)]
        for _ in range(1, NX):
            weights.append(lax.ppermute(weights[-1], "x", pairs))
        gain = prelayer_rms_gain.astype(F32)[None]
        readout = merit_readout[None]

    with jax.named_scope("token_ids"):
        chosen = retained_documents.reshape(-1) - corpus_index * pass_count
        mine = chosen[:, None] == jnp.arange(pass_count, dtype=jnp.int32)[None, :]
        valid = jnp.arange(seq_width, dtype=jnp.int32)[None, :] < document_extent[:, None]
        coded = document_vocab_codes * 2 + valid.astype(jnp.int32)
        coded = jnp.sum(jnp.where(mine[:, :, None], coded[None], 0), axis=1)
        coded = coded.reshape(1, tokens // LANES, LANES)
        coded = swap(jnp.broadcast_to(coded, (NX * NZ, *coded.shape[1:])), CORPUS)
        coded = jnp.sum(coded, axis=0).reshape(tokens)
        token_ids = coded // 2
        token_valid = coded % 2
        lengths = jnp.sum(token_valid.reshape(seq_count, seq_width), axis=1).astype(F32)
        survivor = x_index * n_mp + mp_index
        weight = lax.dynamic_index_in_dim(
            token_valid.reshape(seq_count, seq_width), survivor, 0, keepdims=False
        ).astype(F32) / lax.dynamic_index_in_dim(lengths, survivor, 0, keepdims=False)
        weight = jnp.broadcast_to(weight[:, None], (own_tokens, LANES))

    with jax.named_scope("passage_scores"):
        dots = lax.dot_general(
            question_word_vectors.reshape(-1, vector_dim),
            document_word_vectors.reshape(-1, vector_dim),
            TRANSPOSED,
            preferred_element_type=F32,
        ).reshape(query_count, -1, pass_count, pass_slots)
        slots = jnp.arange(pass_slots, dtype=jnp.int32)[None, :] < document_extent[:, None]
        best = jnp.max(jnp.where(slots[None, None], dots, F32(-1e30)), axis=3)
        scores = jnp.sum(best, axis=1).reshape(-1)
        rider = split3(scores).reshape(1, -1)
        rider = jnp.pad(rider, ((0, 7), (0, width - rider.shape[1])))

    with jax.named_scope("embedded"):
        local_ids = token_ids - corpus_index * vocab_rows
        chosen_rows = (
            local_ids[:, None] == jnp.arange(vocab_rows, dtype=jnp.int32)[None, :]
        ).astype(BF16)
        looked = jnp.dot(chosen_rows, vocab_lookup_table, preferred_element_type=F32).astype(BF16)
        looked = looked.reshape(NX, tokens // NX, width)
        looked = jnp.concatenate([looked, jnp.broadcast_to(rider[None], (NX, 8, width))], axis=1)
        looked = swap(looked, "x")
        rider = looked[:, tokens // NX].reshape(share, LANES)
        looked = jnp.sum(looked[:, : tokens // NX].astype(F32), axis=0).astype(BF16)
        looked = looked.reshape(NZ, share, width)
        looked = jnp.concatenate(
            [looked, jnp.broadcast_to(rider[None], (NZ, *rider.shape))], axis=2
        )
        looked = swap(looked, "z")
        rider = looked[:, :, width:]
        own = jnp.sum(looked[:, :, :width].astype(F32), axis=0)
        rows = share_with(own.astype(BF16), "z", NZ).reshape(-1, width)

    with jax.named_scope("shortlist"):
        table = jnp.sum(rider.reshape(NZ, NX, -1, LANES).astype(F32), axis=2)
        table = table.reshape(NZ, NX, query_count, pass_count)
        table = jnp.transpose(table, (2, 1, 0, 3)).reshape(query_count, -1, LANES)
        at_high = (shortlist_documents // LANES)[:, :, None] == jnp.arange(
            table.shape[1], dtype=jnp.int32
        )
        lines = lax.dot_general(
            at_high.astype(F32), table, (((2,), (1,)), ((0,), (0,))), precision=lax.Precision.HIGHEST
        )
        at_low = (shortlist_documents % LANES)[:, :, None] == jnp.arange(LANES, dtype=jnp.int32)
        picked = jnp.sum(jnp.where(at_low, lines, F32(0.0)), axis=2)
        picked = split3(picked.reshape(-1, LANES)).reshape(-1, LANES)
        pick_rows = picked.shape[0]
        picked = jnp.pad(picked, ((0, 2 * own_tokens - pick_rows), (0, 0)))
        picked = jnp.concatenate([picked[:own_tokens], picked[own_tokens:]], axis=1)

    vmem = pl.BlockSpec(memory_space=pltpu.VMEM)
    params = pltpu.CompilerParams(vmem_limit_bytes=32 << 20)
    own_rows = tokens // NX

    with jax.named_scope("gate_up"):
        part = pl.pallas_call(
            functools.partial(gate_up_kernel, n_mp, units),
            out_shape=jax.ShapeDtypeStruct((n_mp, own_tokens, 2 * half + 2 * LANES), BF16),
            in_specs=[vmem] * 7,
            out_specs=vmem,
            scratch_shapes=[pltpu.VMEM((2 * half, width), BF16), pltpu.VMEM((half, width), BF16)],
            compiler_params=params,
            cost_estimate=pl.CostEstimate(
                flops=4 * own_rows * width * half, bytes_accessed=4 << 20, transcendentals=0
            ),
        )(rows, gain, readout, *weights)
        part = swap(part, "mp")

    with jax.named_scope("hidden"):
        hidden = pl.pallas_call(
            functools.partial(hidden_kernel, n_mp, n_mp * width, half),
            out_shape=jax.ShapeDtypeStruct((own_tokens, half + 2 * LANES), BF16),
            in_specs=[vmem] * 3,
            out_specs=vmem,
            compiler_params=params,
            cost_estimate=pl.CostEstimate(
                flops=own_rows * half * 4, bytes_accessed=2 << 20, transcendentals=own_tokens * half
            ),
        )(part, weight, picked)
        hidden = share_with(hidden, "mp", n_mp)

    with jax.named_scope("down"):
        sent = pl.pallas_call(
            functools.partial(down_kernel, n_mp, units, half),
            out_shape=jax.ShapeDtypeStruct((NZ, share, width + LANES), BF16),
            in_specs=[vmem] * 5,
            out_specs=vmem,
            scratch_shapes=[pltpu.VMEM((half, width), BF16)],
            compiler_params=params,
            cost_estimate=pl.CostEstimate(
                flops=2 * own_rows * width * half, bytes_accessed=4 << 20, transcendentals=0
            ),
        )(hidden, *weights)
        got = swap(sent, "z")
        total = own + jnp.sum(got[:, :, :width].astype(F32), axis=0)
        layer_result = total.astype(BF16)

    with jax.named_scope("results"):
        picked = hidden[:, :, half:].reshape(n_mp, own_tokens, 2, LANES)
        picked = jnp.concatenate([picked[:, :, 0], picked[:, :, 1]], axis=1)[:, :pick_rows]
        picked = jnp.sum(picked.astype(F32).reshape(n_mp, 3, -1, LANES), axis=1)
        shortlist_maxsim = picked.reshape(n_mp * query_count, -1)
        merit = jnp.sum(got[:, :n_mp, width : width + 3].astype(F32), axis=(0, 2))
        merit = jnp.broadcast_to(jnp.pad(merit, (0, LANES - n_mp))[None], (8, LANES))
        merit = share_with(merit, "x", NX)[:, 0, :n_mp]

    return (shortlist_maxsim, layer_result, merit.reshape(retained_documents.shape))


def solution(mesh):
    split = Mesh(mesh.devices.reshape(NX, NZ, -1), ("x", "z", "mp"))
    placed = (
        P("mp", None, None),
        P(CORPUS, None, None),
        P(CORPUS),
        P("mp", None),
        P(),
        P(CORPUS, None),
        P(CORPUS, "mp"),
        P("mp"),
        P("mp", CORPUS),
        P("mp", CORPUS),
        P(CORPUS, "mp"),
        P("mp"),
    )
    return jax.shard_map(
        body, mesh=split, in_specs=placed, out_specs=(P(), P(CORPUS, "mp"), P()), check_vma=False
    )
```

time: 236 us -> 200 us (0.85)
  the two profiles are of different devices: /device:TPU:16 before, /device:TPU:64 now
where the time goes in v2:
time: 200 us; the launch traced here: 199 us
  waiting for transfers between devices  74.1 us (37%)
  starting transfers between devices  60.1 us (30%)
  blocking collectives  30.5 us (15%)
  local copies, waits for them, and re-layouts  11.6 us (6%)
  other arithmetic  10.4 us (5%)
  Pallas kernels  5.95 us (3%)
  matrix products  5.23 us (3%)
    all_to_all x6, waiting for transfers between devices, swap(): return lax.all_to_all(v, axis, 0, 0, tiled=True)  56.6 us
    all_to_all x6, starting transfers between devices, swap(): return lax.all_to_all(v, axis, 0, 0, tiled=True)  53.8 us
    all_to_all x2, blocking collectives, swap(): return lax.all_to_all(v, axis, 0, 0, tiled=True)  30.5 us
    ppermute x3, waiting for transfers between devices, body(): weights.append(lax.ppermute(weights[-1], 'x', pairs))  17.5 us
    ppermute x3, starting transfers between devices, body(): weights.append(lax.ppermute(weights[-1], 'x', pairs))  6.3 us
  transfers between devices with their start and end apart: 9, of which 7 were waited for; matrix products, arithmetic and copies ran while one was open for 8% of the time, Pallas kernels for 0%

profile of v2, /device:TPU:64, one launch (start us, length us, event | category | flops | bytes accessed | tf_op | source)
XLA Modules:
  0.0 198.9 jit_solution(11957613568314897013)
XLA Ops:
  0.6 0.0 copy-start
  0.7 0.8 broadcast_subtract_fusion
  1.5 0.1 copy.38
  1.6 0.1 sub.85
  1.7 0.1 iota_compare_fusion.9
  1.7 0.7 convert_add_fusion
  2.5 0.6 select_reduce_fusion.1
  3.1 0.1 broadcast_in_dim.63
  3.2 0.7 broadcast_in_dim.64
  3.9 17.8 %all-to-all-start = ((s32[64,8,128]{2,1,0:T(8,128)}), s32[64,8,128]{2,1,0:T(8,128)S(1)}, u32[]{:S(2)}, u32[]{:S(2)}) async-start(s32[64,8,128]{2,1,0:T(8,128)} %broadcast_in_dim.64), calls=%async_computation | async-start | bytes 524288 | tf_op jit(solution)/shard_map/token_ids/all_to_all | solution.py:26
  21.6 0.7 iota_compare_fusion.7
  22.4 1.7 select_reduce_fusion
  24.1 0.1 reduce_sum.104
  24.2 0.1 reshape.247
  24.3 16.9 %all-to-all-done = s32[64,8,128]{2,1,0:T(8,128)S(1)} async-done(((s32[64,8,128]{2,1,0:T(8,128)}), s32[64,8,128]{2,1,0:T(8,128)S(1)}, u32[]{:S(2)}, u32[]{:S(2)}) %all-to-all-start) | async-done | bytes 262176 | tf_op jit(solution)/shard_map/token_ids/all_to_all | solution.py:26
  41.2 0.1 reduce_sum.103
  41.3 2.9 %fusion.6 = bf16[1024,512]{1,0:T(8,128)(2,1)S(1)} fusion(bf16[1200,512]{1,0:T(8,128)(2,1)} %param.18, s32[1024]{0:T(1024)S(1)} %fusion.14), kind=kOutput, calls=%fused_computation.6 | convolution fusion | flops 1260044288 | bytes 2281472 | tf_op jit(solution)/shard_map/embedded/dot_general | solution.py:195
  44.2 0.1 pad_maximum_fusion
  44.2 17.7 %all_to_all.40 = bf16[4,264,512]{2,1,0:T(8,128)(2,1)S(1)} all-to-all(bf16[4,264,512]{2,1,0:T(8,128)(2,1)S(1)} %pad_maximum_fusion), channel_id=1, replica_groups=mesh['x'=4,'z'=16,'mp'=8] {'x'}, dimensions={0} | all-to-all | bytes 2162688 | tf_op jit(solution)/shard_map/embedded/all_to_all | solution.py:26
  61.9 0.1 slice_reduce_fusion
  62.1 0.0 copy-start.8
  62.1 0.8 pad_maximum_fusion.2
  62.9 6.0 %all-to-all-start.2 = ((bf16[16,16,640]{2,1,0:T(8,128)(2,1)}), bf16[16,16,640]{2,1,0:T(8,128)(2,1)}, u32[]{:S(2)}, u32[]{:S(2)}) async-start(bf16[16,16,640]{2,1,0:T(8,128)(2,1)} %pad_maximum_fusion.2), calls=%async_computation.2 | async-start | bytes 655360 | tf_op jit(solution)/shard_map/embedded/all_to_all | solution.py:26
  69.0 2.5 %collective-permute-start = (bf16[576,512]{1,0:T(8,128)(2,1)S(1)}, bf16[576,512]{1,0:T(8,128)(2,1)S(1)}, u32[]{:S(2)}, u32[]{:S(2)}) collective-permute-start(bf16[576,512]{1,0:T(8,128)(2,1)S(1)} %pad_maximum_fusion.1.w0_ref), channel_id=1, source_target_pairs={{0,128},{128,256},{256,384},{384,0},{1,129},{129,257},{257,385},{3... | collective-permute-start | bytes 1769480 | tf_op jit(solution)/shard_map/weights/ppermute | solution.py:155
  71.5 13.1 %collective-permute-done.w1_ref = bf16[576,512]{1,0:T(8,128)(2,1)S(1)} collective-permute-done((bf16[576,512]{1,0:T(8,128)(2,1)S(1)}, bf16[576,512]{1,0:T(8,128)(2,1)S(1)}, u32[]{:S(2)}, u32[]{:S(2)}) %collective-permute-start) | collective-permute-done | bytes 589856 | tf_op jit(solution)/shard_map/weights/ppermute | solution.py:155
  84.5 1.9 collective-permute-start.1
  86.4 1.9 all-to-all-done.2
  88.3 1.0 convert_reduce_fusion.1
  89.3 0.6 copy-done.5
  89.9 0.7 broadcast_in_dim.113
  90.6 10.2 %all-to-all-start.3 = ((bf16[16,16,512]{2,1,0:T(8,128)(2,1)}), bf16[16,16,512]{2,1,0:T(8,128)(2,1)S(1)}, u32[]{:S(2)}, u32[]{:S(2)}) async-start(bf16[16,16,512]{2,1,0:T(8,128)(2,1)} %broadcast_in_dim.113), calls=%async_computation.3 | async-start | bytes 524288 | tf_op jit(solution)/shard_map/embedded/all_to_all | solution.py:26
  100.8 1.3 and_select_fusion
  102.2 0.7 reshape.250
  102.8 1.9 collective-permute-start.2
  104.8 0.8 fusion.19
  105.6 0.6 dynamic_slice.9
  106.2 0.7 divide_bitcast_fusion
  106.9 0.9 slice_convert_fusion
  107.7 0.6 bitcast_reduce_fusion
  108.4 1.5 reshape.251
  109.8 1.5 copy.40
  111.3 1.5 reshape.252
  112.8 4.5 %collective-permute-done.2.w3_ref = bf16[576,512]{1,0:T(8,128)(2,1)} collective-permute-done((bf16[576,512]{1,0:T(8,128)(2,1)}, bf16[576,512]{1,0:T(8,128)(2,1)}, u32[]{:S(2)}, u32[]{:S(2)}) %collective-permute-start.2) | collective-permute-done | bytes 589856 | tf_op jit(solution)/shard_map/weights/ppermute | solution.py:155
  117.3 2.0 %gate_up.1 = bf16[8,32,1792]{2,1,0:T(8,128)(2,1)S(1)} custom-call(bf16[256,512]{1,0:T(8,128)(2,1)S(1)} %bitcast.59, f32[1,512]{1,0:T(1,128)S(1)} %bitcast.60, f32[1,512]{1,0:T(1,128)S(1)} %bitcast.61, bf16[576,512]{1,0:T(8,128)(2,1)S(1)} %pad_maximum_fusion.1.w0_ref, bf16[576,512]{1,0:T(8,128)(2,1)S(1)} %collective-permute-done.w1_ref, ...), custom_call_target="tpu_custom_call" | custom-call | flops 402653184 | bytes 4194304 | tf_op jit(solution)/shard_map/gate_up/pallas_call | solution.py:232
  119.4 1.0 copy-done.1
  120.3 4.6 %all-to-all-start.4 = ((bf16[8,32,1792]{2,1,0:T(8,128)(2,1)}), bf16[8,32,1792]{2,1,0:T(8,128)(2,1)}, u32[]{:S(2)}, u32[]{:S(2)}) async-start(bf16[8,32,1792]{2,1,0:T(8,128)(2,1)} %copy-done.1), calls=%async_computation.4 | async-start | bytes 1835008 | tf_op jit(solution)/shard_map/gate_up/all_to_all | solution.py:26
  124.9 0.7 fusion.7
  125.7 13.8 %all-to-all-done.4.got_ref = bf16[8,32,1792]{2,1,0:T(8,128)(2,1)} async-done(((bf16[8,32,1792]{2,1,0:T(8,128)(2,1)}), bf16[8,32,1792]{2,1,0:T(8,128)(2,1)}, u32[]{:S(2)}, u32[]{:S(2)}) %all-to-all-start.4) | async-done | bytes 917536 | tf_op jit(solution)/shard_map/gate_up/all_to_all | solution.py:26
  139.6 0.1 broadcast_in_dim.117.weight_ref
  139.6 1.6 hidden.1
  141.2 0.1 broadcast_in_dim.119
  141.3 12.8 %all_to_all.41.got_ref = bf16[8,32,1024]{2,1,0:T(8,128)(2,1)S(1)} all-to-all(bf16[8,32,1024]{2,1,0:T(8,128)(2,1)S(1)} %broadcast_in_dim.119), channel_id=1, replica_groups=mesh['x'=4,'z'=16,'mp'=8] {'mp'}, dimensions={0} | all-to-all | bytes 1048576 | tf_op jit(solution)/shard_map/hidden/all_to_all | solution.py:26
  154.1 2.3 %down.1 = bf16[16,16,640]{2,1,0:T(8,128)(2,1)} custom-call(bf16[8,32,1024]{2,1,0:T(8,128)(2,1)S(1)} %all_to_all.41.got_ref, bf16[576,512]{1,0:T(8,128)(2,1)S(1)} %pad_maximum_fusion.1.w0_ref, bf16[576,512]{1,0:T(8,128)(2,1)S(1)} %copy-done.3, bf16[576,512]{1,0:T(8,128)(2,1)} %collective-permute-done.1.w2_ref, bf16[576,512]{1,0:T(8,128)(2,1)} %collective-permute-done.2.w3_ref), custom_call_target="tpu_custom_call" | custom-call | flops 201326592 | bytes 4194304 | tf_op jit(solution)/shard_map/down/pallas_call | solution.py:259
  156.5 12.0 %all-to-all-start.6 = ((bf16[16,16,640]{2,1,0:T(8,128)(2,1)}), bf16[16,16,640]{2,1,0:T(8,128)(2,1)S(1)}, u32[]{:S(2)}, u32[]{:S(2)}) async-start(bf16[16,16,640]{2,1,0:T(8,128)(2,1)} %down.1), calls=%async_computation.6 | async-start | bytes 655360 | tf_op jit(solution)/shard_map/down/all_to_all | solution.py:26
  168.6 0.2 fusion.20
  168.9 0.6 reshape.257
  169.5 19.3 %all-to-all-done.6 = bf16[16,16,640]{2,1,0:T(8,128)(2,1)S(1)} async-done(((bf16[16,16,640]{2,1,0:T(8,128)(2,1)}), bf16[16,16,640]{2,1,0:T(8,128)(2,1)S(1)}, u32[]{:S(2)}, u32[]{:S(2)}) %all-to-all-start.6) | async-done | bytes 327712 | tf_op jit(solution)/shard_map/down/all_to_all | solution.py:26
  188.9 0.1 convert_reduce_fusion.3
  189.0 0.6 broadcast_in_dim.120
  189.6 3.2 %all-to-all-start.7 = ((f32[4,8,128]{2,1,0:T(8,128)}), f32[4,8,128]{2,1,0:T(8,128)S(1)}, u32[]{:S(2)}, u32[]{:S(2)}) async-start(f32[4,8,128]{2,1,0:T(8,128)} %broadcast_in_dim.120), calls=%async_computation.7 | async-start | bytes 32768 | tf_op jit(solution)/shard_map/results/all_to_all | solution.py:26
  192.9 0.6 add_convert_fusion
  193.5 4.7 %all-to-all-done.7 = f32[4,8,128]{2,1,0:T(8,128)S(1)} async-done(((f32[4,8,128]{2,1,0:T(8,128)}), f32[4,8,128]{2,1,0:T(8,128)S(1)}, u32[]{:S(2)}, u32[]{:S(2)}) %all-to-all-start.7) | async-done | bytes 16416 | tf_op jit(solution)/shard_map/results/all_to_all | solution.py:26
  198.2 0.1 squeeze.19
  198.3 0.6 copy.43
  (53 shorter events, 0.4 us)
Async XLA Ops:
  0.6 21.8 %copy-start = (bf16[64,128,128]{2,1,0:T(8,128)(2,1)S(1)}, bf16[64,128,128]{2,1,0:T(8,128)(2,1)}, u32[]{:S(2)}) copy-start(bf16[64,128,128]{2,1,0:T(8,128)(2,1)} %param.13) | copy-start | bytes 6291460
  3.9 37.3 %all-to-all-start = ((s32[64,8,128]{2,1,0:T(8,128)}), s32[64,8,128]{2,1,0:T(8,128)S(1)}, u32[]{:S(2)}, u32[]{:S(2)}) async-start(s32[64,8,128]{2,1,0:T(8,128)} %broadcast_in_dim.64), calls=%async_computation | async-start | bytes 524288 | tf_op jit(solution)/shard_map/token_ids/all_to_all | solution.py:26
  61.9 7.0 %copy-start.7 = (bf16[192,512]{1,0:T(8,128)(2,1)S(1)}, bf16[192,512]{1,0:T(8,128)(2,1)}, u32[]{:S(2)}) copy-start(bf16[192,512]{1,0:T(8,128)(2,1)} %param.22) | copy-start | bytes 589828
  62.1 6.8 %copy-start.8 = (bf16[512,192]{0,1:T(8,128)(2,1)S(1)}, bf16[512,192]{0,1:T(8,128)(2,1)}, u32[]{:S(2)}) copy-start(bf16[512,192]{0,1:T(8,128)(2,1)} %param.21) | copy-start | bytes 589828
  62.1 6.8 %copy-start.9 = (bf16[512,192]{0,1:T(8,128)(2,1)S(1)}, bf16[512,192]{0,1:T(8,128)(2,1)}, u32[]{:S(2)}) copy-start(bf16[512,192]{0,1:T(8,128)(2,1)} %param.20) | copy-start | bytes 589828
  62.9 25.4 %all-to-all-start.2 = ((bf16[16,16,640]{2,1,0:T(8,128)(2,1)}), bf16[16,16,640]{2,1,0:T(8,128)(2,1)}, u32[]{:S(2)}, u32[]{:S(2)}) async-start(bf16[16,16,640]{2,1,0:T(8,128)(2,1)} %pad_maximum_fusion.2), calls=%async_computation.2 | async-start | bytes 655360 | tf_op jit(solution)/shard_map/embedded/all_to_all | solution.py:26
  68.9 31.9 %copy-start.13 = (bf16[512]{0:T(512)(128)(2,1)S(1)}, bf16[512]{0:T(512)(128)(2,1)}, u32[]{:S(2)}) copy-start(bf16[512]{0:T(512)(128)(2,1)} %param.19) | copy-start | bytes 3076
  69.0 48.3 %copy-start.4 = (f32[512]{0:T(512)S(1)}, f32[512]{0:T(512)}, u32[]{:S(2)}) copy-start(f32[512]{0:T(512)} %param.23) | copy-start | bytes 6148
  69.0 15.5 %collective-permute-start = (bf16[576,512]{1,0:T(8,128)(2,1)S(1)}, bf16[576,512]{1,0:T(8,128)(2,1)S(1)}, u32[]{:S(2)}, u32[]{:S(2)}) collective-permute-start(bf16[576,512]{1,0:T(8,128)(2,1)S(1)} %pad_maximum_fusion.1.w0_ref), channel_id=1, source_target_pairs={{0,128},{128,256},{256,384},{384,0},{1,129},{129,257},{257,385},{3... | collective-permute-start | bytes 1769480 | tf_op jit(solution)/shard_map/weights/ppermute | solution.py:155
  84.5 34.8 %copy-start.2 = (bf16[576,512]{1,0:T(8,128)(2,1)}, bf16[576,512]{1,0:T(8,128)(2,1)S(1)}, u32[]{:S(2)}) copy-start(bf16[576,512]{1,0:T(8,128)(2,1)S(1)} %collective-permute-done.w1_ref) | copy-start | bytes 1769476
  84.5 18.3 %collective-permute-start.1 = (bf16[576,512]{1,0:T(8,128)(2,1)S(1)}, bf16[576,512]{1,0:T(8,128)(2,1)}, u32[]{:S(2)}, u32[]{:S(2)}) collective-permute-start(bf16[576,512]{1,0:T(8,128)(2,1)S(1)} %collective-permute-done.w1_ref), channel_id=1, source_target_pairs={{0,128},{128,256},{256,384},{384,0},{1,129},{129,257},{257,385},{3... | collective-permute-start | bytes 1769480 | tf_op jit(solution)/shard_map/weights/ppermute | solution.py:155
  89.3 0.6 copy-start.5
  90.6 26.7 %all-to-all-start.3 = ((bf16[16,16,512]{2,1,0:T(8,128)(2,1)}), bf16[16,16,512]{2,1,0:T(8,128)(2,1)S(1)}, u32[]{:S(2)}, u32[]{:S(2)}) async-start(bf16[16,16,512]{2,1,0:T(8,128)(2,1)} %broadcast_in_dim.113), calls=%async_computation.3 | async-start | bytes 524288 | tf_op jit(solution)/shard_map/embedded/all_to_all | solution.py:26
  102.8 14.5 %collective-permute-start.2 = (bf16[576,512]{1,0:T(8,128)(2,1)}, bf16[576,512]{1,0:T(8,128)(2,1)}, u32[]{:S(2)}, u32[]{:S(2)}) collective-permute-start(bf16[576,512]{1,0:T(8,128)(2,1)} %collective-permute-done.1.w2_ref), channel_id=1, source_target_pairs={{0,128},{128,256},{256,384},{384,0},{1,129},{129,257},{257,385},{3... | collective-permute-start | bytes 1769480 | tf_op jit(solution)/shard_map/weights/ppermute | solution.py:155
  119.3 1.0 copy-start.1
  120.3 4.6 %copy-start.10 = (f32[2,32,128]{2,1,0:T(8,128)S(1)}, f32[2,32,128]{2,1,0:T(8,128)}, u32[]{:S(2)}) copy-start(f32[2,32,128]{2,1,0:T(8,128)} %reshape.252) | copy-start | bytes 98308
  120.3 4.6 %copy-start.11 = (s32[2,1024]{1,0:T(2,128)S(1)}, s32[2,1024]{1,0:T(2,128)}, u32[]{:S(2)}) copy-start(s32[2,1024]{1,0:T(2,128)} %get-tuple-element.25) | copy-start | bytes 24580
  120.3 4.6 %copy-start.12 = (s32[2,1024]{1,0:T(2,128)S(1)}, s32[2,1024]{1,0:T(2,128)}, u32[]{:S(2)}) copy-start(s32[2,1024]{1,0:T(2,128)} %get-tuple-element.26) | copy-start | bytes 24580
  120.3 19.3 %all-to-all-start.4 = ((bf16[8,32,1792]{2,1,0:T(8,128)(2,1)}), bf16[8,32,1792]{2,1,0:T(8,128)(2,1)}, u32[]{:S(2)}, u32[]{:S(2)}) async-start(bf16[8,32,1792]{2,1,0:T(8,128)(2,1)} %copy-done.1), calls=%async_computation.4 | async-start | bytes 1835008 | tf_op jit(solution)/shard_map/gate_up/all_to_all | solution.py:26
  139.6 14.5 %copy-start.3 = (bf16[576,512]{1,0:T(8,128)(2,1)S(1)}, bf16[576,512]{1,0:T(8,128)(2,1)}, u32[]{:S(2)}) copy-start(bf16[576,512]{1,0:T(8,128)(2,1)} %copy-done.2) | copy-start | bytes 1769476
  156.5 32.4 %all-to-all-start.6 = ((bf16[16,16,640]{2,1,0:T(8,128)(2,1)}), bf16[16,16,640]{2,1,0:T(8,128)(2,1)S(1)}, u32[]{:S(2)}, u32[]{:S(2)}) async-start(bf16[16,16,640]{2,1,0:T(8,128)(2,1)} %down.1), calls=%async_computation.6 | async-start | bytes 655360 | tf_op jit(solution)/shard_map/down/all_to_all | solution.py:26
  168.5 24.4 %copy-start.6 = (f32[16,512]{1,0:T(8,128)S(1)}, f32[16,512]{1,0:T(8,128)}, u32[]{:S(2)}) copy-start(f32[16,512]{1,0:T(8,128)} %copy-done.5) | copy-start | bytes 98308
  189.6 8.6 %all-to-all-start.7 = ((f32[4,8,128]{2,1,0:T(8,128)}), f32[4,8,128]{2,1,0:T(8,128)S(1)}, u32[]{:S(2)}, u32[]{:S(2)}) async-start(f32[4,8,128]{2,1,0:T(8,128)} %broadcast_in_dim.120), calls=%async_computation.7 | async-start | bytes 32768 | tf_op jit(solution)/shard_map/results/all_to_all | solution.py:26

commit v3 on v2

--- a/solution.py
+++ b/solution.py
@@ -44,15 +44,73 @@
     return block
 
 
+def ids_kernel(base_ref, chosen_ref, extent_ref, codes_ref, out_ref, wide, tile):
+    slots, passes = codes_ref.shape
+    each = LANES // slots
+    wide[...] = jnp.concatenate([codes_ref[...]] * each, axis=0).T
+    lane = lax.broadcasted_iota(jnp.int32, (1, LANES), 1)
+    for row in range(tile.shape[0]):
+        line = jnp.zeros((1, LANES), jnp.int32)
+        for part in range(each):
+            survivor = row * each + part
+            kept = chosen_ref.shape[0]
+            index = chosen_ref[survivor % kept, survivor // kept] - base_ref[0]
+            held = (index >= 0) & (index < passes)
+            index = jnp.clip(index, 0, passes - 1)
+            first = part * slots
+            here = (lane >= first) & (lane < jnp.where(held, first + slots, first))
+            valid = (lane < first + extent_ref[index]).astype(jnp.int32)
+            line = jnp.where(here, wide[pl.ds(index, 1), :] * 2 + valid, line)
+        tile[row : row + 1, :] = line
+    out_ref[...] = jnp.broadcast_to(tile[...][None], out_ref.shape)
+
+
+def own_kernel(got_ref, own_ref, rows_ref, table_ref):
+    width = own_ref.shape[1]
+    total = got_ref[0, :, :width].astype(F32)
+    for source in range(1, got_ref.shape[0]):
+        total += got_ref[source, :, :width].astype(F32)
+    own_ref[...] = total
+    rows_ref[...] = jnp.broadcast_to(total.astype(BF16)[None], rows_ref.shape)
+    scores = got_ref[:, :, width:].astype(F32)
+    each = scores.shape[1] // NX
+    queries = table_ref.shape[0]
+    passes = LANES // queries
+    lines = scores.shape[0] // queries
+    for i in range(NX):
+        value = jnp.sum(scores[:, i * each : (i + 1) * each], axis=1)
+        value = value.reshape(lines, queries, LANES)
+        for query in range(queries):
+            take = slice(query * passes, (query + 1) * passes)
+            table_ref[query, i * lines : (i + 1) * lines, :] = jnp.concatenate(
+                [value[:, j, take] for j in range(queries)], axis=1
+            )
+
+
+def gather_rows(parts, start, stop, into, at):
+    *whole, low, high = parts
+    for part in whole:
+        into[at : at + stop - start, :] = part[start:stop, :]
+        at += stop - start
+    middle = low.shape[0]
+    if start < middle:
+        end = min(stop, middle)
+        into[at : at + end - start, :] = low[start:end, :]
+        at += end - start
+    if stop > middle:
+        begin = max(start, middle)
+        into[at : at + stop - begin, :] = high[begin - middle : stop - middle, :]
+
+
 def gate_up_kernel(
-    n_mp, units, rows_ref, gain_ref, readout_ref, w0_ref, w1_ref, w2_ref, w3_ref, out_ref, first, second
+    n_mp, units, rows_ref, gain_ref, readout_ref, w0_ref, w1_ref, w2_ref, w3_ref, w4_ref, out_ref,
+    first, second,
 ):
-    parts = (w0_ref, w1_ref, w2_ref, w3_ref)
+    parts = (w0_ref, w1_ref, w2_ref, w3_ref, w4_ref)
     half = NX * units
-    for i, part in enumerate(parts):
-        first[i * units : (i + 1) * units, :] = part[:units, :]
-        first[half + i * units : half + (i + 1) * units, :] = part[units : 2 * units, :]
-        second[i * units : (i + 1) * units, :] = part[2 * units :, :]
+    gather_rows(parts, 0, units, first, 0)
+    gather_rows(parts, units, 2 * units, first, half)
+    gather_rows(parts, 2 * units, 3 * units, second, 0)
     value = rows_ref[...].astype(F32)
     squares = jnp.sum(value * value, axis=1, keepdims=True)
     reading = jnp.sum(value * readout_ref[...], axis=1, keepdims=True)
@@ -104,15 +162,26 @@
     out_ref[:, half + LANES :] = rider.astype(BF16)
 
 
-def down_kernel(n_mp, units, half, got_ref, w0_ref, w1_ref, w2_ref, w3_ref, out_ref, second):
-    for i, part in enumerate((w0_ref, w1_ref, w2_ref, w3_ref)):
-        second[i * units : (i + 1) * units, :] = part[2 * units :, :]
+def down_kernel(
+    n_mp, units, half, got_ref, w0_ref, w1_ref, w2_ref, w3_ref, w4_ref, out_ref, picks_ref, second
+):
+    parts = (w0_ref, w1_ref, w2_ref, w3_ref, w4_ref)
+    gather_rows(parts, 2 * units, 3 * units, second, 0)
     tokens = got_ref.shape[0] * got_ref.shape[1]
     hidden = got_ref[:, :, :half].reshape(tokens, half)
     down = jnp.dot(hidden, second[...], preferred_element_type=F32)
     groups = out_ref.shape[0]
     share = tokens // groups
     shares = got_ref[:, 16:, half + LANES :].astype(F32)
+    whole = got_ref[:, :, half : half + LANES].astype(F32)
+    last = got_ref[:, :16, half + LANES :].astype(F32)
+    picks = whole[:, :16] + whole[:, 16:] + last
+    lines = picks_ref.shape[1] // LANES
+    for i in range(picks_ref.shape[0]):
+        at = i * lines % picks.shape[1]
+        picks_ref[i : i + 1, :] = jnp.concatenate(
+            [picks[i * lines // picks.shape[1], at + j : at + j + 1] for j in range(lines)], axis=1
+        )
     rider = fill((n_mp, LANES), 1, (shares[:, 0], shares[:, 1], shares[:, 2]))
     rider = jnp.concatenate([rider, jnp.zeros((share - n_mp, LANES), F32)], axis=0).astype(BF16)
     for target in range(groups):
@@ -147,32 +216,32 @@
     tokens = seq_count * seq_width
     share = tokens // (NX * NZ)
     own_tokens = tokens // NX // n_mp
+    vmem = pl.BlockSpec(memory_space=pltpu.VMEM)
+    smem = pl.BlockSpec(memory_space=pltpu.SMEM)
 
     with jax.named_scope("weights"):
         weights = [jnp.concatenate([gating_projector.T, widening_projector.T, reducing_projector], axis=0)]
-        pairs = [(i, (i + 1) % NX) for i in range(NX)]
-        for _ in range(1, NX):
-            weights.append(lax.ppermute(weights[-1], "x", pairs))
+        up = [(i, (i + 1) % NX) for i in range(NX)]
+        down = [(i, (i - 1) % NX) for i in range(NX)]
+        weights += [lax.ppermute(weights[0], "x", up), lax.ppermute(weights[0], "x", down)]
         gain = prelayer_rms_gain.astype(F32)[None]
         readout = merit_readout[None]
 
     with jax.named_scope("token_ids"):
-        chosen = retained_documents.reshape(-1) - corpus_index * pass_count
-        mine = chosen[:, None] == jnp.arange(pass_count, dtype=jnp.int32)[None, :]
-        valid = jnp.arange(seq_width, dtype=jnp.int32)[None, :] < document_extent[:, None]
-        coded = document_vocab_codes * 2 + valid.astype(jnp.int32)
-        coded = jnp.sum(jnp.where(mine[:, :, None], coded[None], 0), axis=1)
-        coded = coded.reshape(1, tokens // LANES, LANES)
-        coded = swap(jnp.broadcast_to(coded, (NX * NZ, *coded.shape[1:])), CORPUS)
+        base = (corpus_index * pass_count).astype(jnp.int32).reshape(1)
+        coded = pl.pallas_call(
+            ids_kernel,
+            out_shape=jax.ShapeDtypeStruct((NX * NZ, tokens // LANES, LANES), jnp.int32),
+            in_specs=[smem] * 3 + [vmem],
+            out_specs=vmem,
+            scratch_shapes=[
+                pltpu.VMEM((pass_count, LANES), jnp.int32),
+                pltpu.VMEM((tokens // LANES, LANES), jnp.int32),
+            ],
+        )(base, retained_documents.T, document_extent, document_vocab_codes.T)
+        coded = swap(coded, CORPUS)
         coded = jnp.sum(coded, axis=0).reshape(tokens)
         token_ids = coded // 2
-        token_valid = coded % 2
-        lengths = jnp.sum(token_valid.reshape(seq_count, seq_width), axis=1).astype(F32)
-        survivor = x_index * n_mp + mp_index
-        weight = lax.dynamic_index_in_dim(
-            token_valid.reshape(seq_count, seq_width), survivor, 0, keepdims=False
-        ).astype(F32) / lax.dynamic_index_in_dim(lengths, survivor, 0, keepdims=False)
-        weight = jnp.broadcast_to(weight[:, None], (own_tokens, LANES))
 
     with jax.named_scope("passage_scores"):
         dots = lax.dot_general(
@@ -203,28 +272,22 @@
             [looked, jnp.broadcast_to(rider[None], (NZ, *rider.shape))], axis=2
         )
         looked = swap(looked, "z")
-        rider = looked[:, :, width:]
-        own = jnp.sum(looked[:, :, :width].astype(F32), axis=0)
-        rows = share_with(own.astype(BF16), "z", NZ).reshape(-1, width)
-
-    with jax.named_scope("shortlist"):
-        table = jnp.sum(rider.reshape(NZ, NX, -1, LANES).astype(F32), axis=2)
-        table = table.reshape(NZ, NX, query_count, pass_count)
-        table = jnp.transpose(table, (2, 1, 0, 3)).reshape(query_count, -1, LANES)
-        at_high = (shortlist_documents // LANES)[:, :, None] == jnp.arange(
-            table.shape[1], dtype=jnp.int32
-        )
-        lines = lax.dot_general(
-            at_high.astype(F32), table, (((2,), (1,)), ((0,), (0,))), precision=lax.Precision.HIGHEST
-        )
-        at_low = (shortlist_documents % LANES)[:, :, None] == jnp.arange(LANES, dtype=jnp.int32)
-        picked = jnp.sum(jnp.where(at_low, lines, F32(0.0)), axis=2)
-        picked = split3(picked.reshape(-1, LANES)).reshape(-1, LANES)
-        pick_rows = picked.shape[0]
-        picked = jnp.pad(picked, ((0, 2 * own_tokens - pick_rows), (0, 0)))
-        picked = jnp.concatenate([picked[:own_tokens], picked[own_tokens:]], axis=1)
-
-    vmem = pl.BlockSpec(memory_space=pltpu.VMEM)
+        own, rows, table = pl.pallas_call(
+            own_kernel,
+            out_shape=(
+                jax.ShapeDtypeStruct((share, width), F32),
+                jax.ShapeDtypeStruct((NZ, share, width), BF16),
+                jax.ShapeDtypeStruct((query_count, NX * NZ * pass_count // LANES, LANES), F32),
+            ),
+            in_specs=[vmem],
+            out_specs=(vmem, vmem, vmem),
+        )(looked)
+        rows, *weights = lax.optimization_barrier((rows, *weights))
+        middle = weights[0].shape[0] // 2
+        weights.append(lax.ppermute(weights[1][:middle], "x", up))
+        weights.append(lax.ppermute(weights[2][middle:], "x", down))
+        rows = swap(rows, "z").reshape(-1, width)
+
     params = pltpu.CompilerParams(vmem_limit_bytes=32 << 20)
     own_rows = tokens // NX
 
@@ -232,7 +295,7 @@
         part = pl.pallas_call(
             functools.partial(gate_up_kernel, n_mp, units),
             out_shape=jax.ShapeDtypeStruct((n_mp, own_tokens, 2 * half + 2 * LANES), BF16),
-            in_specs=[vmem] * 7,
+            in_specs=[vmem] * 8,
             out_specs=vmem,
             scratch_shapes=[pltpu.VMEM((2 * half, width), BF16), pltpu.VMEM((half, width), BF16)],
             compiler_params=params,
@@ -240,7 +303,30 @@
                 flops=4 * own_rows * width * half, bytes_accessed=4 << 20, transcendentals=0
             ),
         )(rows, gain, readout, *weights)
+        part, coded, table = lax.optimization_barrier((part, coded, table))
         part = swap(part, "mp")
+
+    with jax.named_scope("token_weights"):
+        token_valid = coded % 2
+        lengths = jnp.sum(token_valid.reshape(seq_count, seq_width), axis=1).astype(F32)
+        survivor = x_index * n_mp + mp_index
+        weight = lax.dynamic_index_in_dim(
+            token_valid.reshape(seq_count, seq_width), survivor, 0, keepdims=False
+        ).astype(F32) / lax.dynamic_index_in_dim(lengths, survivor, 0, keepdims=False)
+        weight = jnp.broadcast_to(weight[:, None], (own_tokens, LANES))
+
+    with jax.named_scope("shortlist"):
+        at_high = (shortlist_documents // LANES)[:, :, None] == jnp.arange(
+            table.shape[1], dtype=jnp.int32
+        )
+        lines = lax.dot_general(
+            at_high.astype(F32), table, (((2,), (1,)), ((0,), (0,))), precision=lax.Precision.HIGHEST
+        )
+        at_low = (shortlist_documents % LANES)[:, :, None] == jnp.arange(LANES, dtype=jnp.int32)
+        picked = jnp.sum(jnp.where(at_low, lines, F32(0.0)), axis=2)
+        picked = split3(picked.reshape(-1, LANES)).reshape(-1, LANES)
+        picked = jnp.pad(picked, ((0, 2 * own_tokens - picked.shape[0]), (0, 0)))
+        picked = jnp.concatenate([picked[:own_tokens], picked[own_tokens:]], axis=1)
 
     with jax.named_scope("hidden"):
         hidden = pl.pallas_call(
@@ -256,11 +342,14 @@
         hidden = share_with(hidden, "mp", n_mp)
 
     with jax.named_scope("down"):
-        sent = pl.pallas_call(
+        sent, shortlist_maxsim = pl.pallas_call(
             functools.partial(down_kernel, n_mp, units, half),
-            out_shape=jax.ShapeDtypeStruct((NZ, share, width + LANES), BF16),
-            in_specs=[vmem] * 5,
-            out_specs=vmem,
+            out_shape=(
+                jax.ShapeDtypeStruct((NZ, share, width + LANES), BF16),
+                jax.ShapeDtypeStruct((n_mp * query_count, shortlist_documents.shape[1]), F32),
+            ),
+            in_specs=[vmem] * 6,
+            out_specs=(vmem, vmem),
             scratch_shapes=[pltpu.VMEM((half, width), BF16)],
             compiler_params=params,
             cost_estimate=pl.CostEstimate(
@@ -272,10 +361,6 @@
         layer_result = total.astype(BF16)
 
     with jax.named_scope("results"):
-        picked = hidden[:, :, half:].reshape(n_mp, own_tokens, 2, LANES)
-        picked = jnp.concatenate([picked[:, :, 0], picked[:, :, 1]], axis=1)[:, :pick_rows]
-        picked = jnp.sum(picked.astype(F32).reshape(n_mp, 3, -1, LANES), axis=1)
-        shortlist_maxsim = picked.reshape(n_mp * query_count, -1)
         merit = jnp.sum(got[:, :n_mp, width : width + 3].astype(F32), axis=(0, 2))
         merit = jnp.broadcast_to(jnp.pad(merit, (0, LANES - n_mp))[None], (8, LANES))
         merit = share_with(merit, "x", NX)[:, 0, :n_mp]

time: 200 us -> 195 us (0.975)
  blocking collectives: 30.5 us -> 62.6 us
  waiting for transfers between devices: 74.1 us -> 52.2 us
  starting transfers between devices: 60.1 us -> 52.6 us
  local copies, waits for them, and re-layouts: 11.6 us -> 5.74 us
  other arithmetic: 10.4 us -> 4.88 us
  Pallas kernels: 5.95 us -> 9.3 us
    all_to_all x2 -> x3, blocking collectives: 30.5 us -> 62.6 us  [swap(): return lax.all_to_all(v, axis, 0, 0, tiled=True)]
    all_to_all x6 -> x5, starting transfers between devices: 53.8 us -> 41 us  [swap(): return lax.all_to_all(v, axis, 0, 0, tiled=True)]
    ppermute x3 -> x4, waiting for transfers between devices: 17.5 us -> 4.86 us  [the longest x1 3.14 us: body(): weights.append(lax.ppermute(weights[1][:middle], 'x', up))]
    all_to_all x6 -> x5, waiting for transfers between devices: 56.6 us -> 47.4 us  [swap(): return lax.all_to_all(v, axis, 0, 0, tiled=True)]
    ppermute x3 -> x4, starting transfers between devices: 6.3 us -> 11.7 us  [the longest x1 3.92 us: body(): weights.append(lax.ppermute(weights[1][:middle], 'x', up))]
    reshape x5 -> x1, local copies, waits for them, and re-layouts: 4.37 us -> 0.07 us  [body(): token_valid.reshape(seq_count, seq_width)]
    pallas_call x0 -> x2, Pallas kernels: none -> 3.55 us  [the longest x1 1.81 us: body(): pl.pallas_call(own_kernel, out_shape=(jax.ShapeDtypeStruct((share, width)...]
    reduce_sum x4 -> x0, other arithmetic: 2.27 us -> none  [the longest x1 1 us: body(): own = jnp.sum(looked[:, :, :width].astype(F32), axis=0)]
  transfers between devices with their start and end apart: 9 -> 9, of which waited for: 7 -> 6; matrix products, arithmetic and copies ran while one was open for 8% -> 5% of each run, Pallas kernels for 0% -> 1%
where the time goes in v3:
time: 195 us; the launch traced here: 194 us
  blocking collectives  62.6 us (32%)
  starting transfers between devices  52.6 us (27%)
  waiting for transfers between devices  52.2 us (27%)
  Pallas kernels  9.3 us (5%)
  local copies, waits for them, and re-layouts  5.74 us (3%)
  matrix products  5.22 us (3%)
  other arithmetic  4.88 us (3%)
    all_to_all x3, blocking collectives, swap(): return lax.all_to_all(v, axis, 0, 0, tiled=True)  62.6 us
    all_to_all x5, waiting for transfers between devices, swap(): return lax.all_to_all(v, axis, 0, 0, tiled=True)  47.4 us
    all_to_all x5, starting transfers between devices, swap(): return lax.all_to_all(v, axis, 0, 0, tiled=True)  41 us
    ppermute x1, starting transfers between devices, body(): weights.append(lax.ppermute(weights[1][:middle], 'x', up))  3.92 us
  transfers between devices with their start and end apart: 9, of which 6 were waited for; matrix products, arithmetic and copies ran while one was open for 5% of the time, Pallas kernels for 1%

profile of v3, /device:TPU:64, one launch (start us, length us, event | category | flops | bytes accessed | tf_op | source)
XLA Modules:
  0.0 193.7 jit_solution(10911310989669829078)
XLA Ops:
  0.6 0.0 copy-start
  0.7 1.7 token_ids.1
  2.4 17.8 %all-to-all-start = ((s32[64,8,128]{2,1,0:T(8,128)}), s32[64,8,128]{2,1,0:T(8,128)S(1)}, u32[]{:S(2)}, u32[]{:S(2)}) async-start(s32[64,8,128]{2,1,0:T(8,128)} %token_ids.1), calls=%async_computation | async-start | bytes 524288 | tf_op jit(solution)/shard_map/token_ids/all_to_all | solution.py:26
  20.2 0.7 iota_compare_fusion.7
  20.9 0.0 copy-done
  20.9 1.7 select_reduce_fusion
  22.6 0.1 reduce_sum.67
  22.7 0.1 reshape.196
  22.8 16.9 %all-to-all-done = s32[64,8,128]{2,1,0:T(8,128)S(1)} async-done(((s32[64,8,128]{2,1,0:T(8,128)}), s32[64,8,128]{2,1,0:T(8,128)S(1)}, u32[]{:S(2)}, u32[]{:S(2)}) %all-to-all-start) | async-done | bytes 262176 | tf_op jit(solution)/shard_map/token_ids/all_to_all | solution.py:26
  39.7 0.1 reduce_sum.66
  39.8 2.9 %fusion.6 = bf16[1024,512]{1,0:T(8,128)(2,1)S(1)} fusion(bf16[1200,512]{1,0:T(8,128)(2,1)} %param.18, s32[1024]{0:T(1024)S(1)} %fusion.13), kind=kOutput, calls=%fused_computation.6 | convolution fusion | flops 1260044288 | bytes 2281472 | tf_op jit(solution)/shard_map/embedded/dot_general | solution.py:264
  42.7 0.1 pad_maximum_fusion
  42.7 17.7 %all_to_all.40 = bf16[4,264,512]{2,1,0:T(8,128)(2,1)S(1)} all-to-all(bf16[4,264,512]{2,1,0:T(8,128)(2,1)S(1)} %pad_maximum_fusion), channel_id=1, replica_groups=mesh['x'=4,'z'=16,'mp'=8] {'x'}, dimensions={0} | all-to-all | bytes 2162688 | tf_op jit(solution)/shard_map/embedded/all_to_all | solution.py:26
  60.5 0.1 slice_reduce_fusion
  60.6 0.0 copy-start.4
  60.6 0.0 copy-start.5
  60.7 0.8 pad_maximum_fusion.2
  61.4 6.0 %all-to-all-start.2 = ((bf16[16,16,640]{2,1,0:T(8,128)(2,1)}), bf16[16,16,640]{2,1,0:T(8,128)(2,1)}, u32[]{:S(2)}, u32[]{:S(2)}) async-start(bf16[16,16,640]{2,1,0:T(8,128)(2,1)} %pad_maximum_fusion.2), calls=%async_computation.2 | async-start | bytes 655360 | tf_op jit(solution)/shard_map/embedded/all_to_all | solution.py:26
  67.4 0.0 copy-done.3
  67.4 0.0 copy-done.4
  67.4 0.0 copy-done.5
  67.5 0.0 copy-start.9
  67.5 0.0 copy-start.2
  67.5 3.1 %collective-permute-start.1 = (bf16[576,512]{1,0:T(8,128)(2,1)S(1)}, bf16[576,512]{1,0:T(8,128)(2,1)S(1)}, u32[]{:S(2)}, u32[]{:S(2)}) collective-permute-start(bf16[576,512]{1,0:T(8,128)(2,1)S(1)} %pad_maximum_fusion.1.w0_ref), channel_id=1, source_target_pairs={{0,384},{128,0},{256,128},{384,256},{1,385},{129,1},{257,129},{385... | collective-permute-start | bytes 1769480 | tf_op jit(solution)/shard_map/weights/ppermute | solution.py:226
  70.6 2.8 %collective-permute-start = (bf16[576,512]{1,0:T(8,128)(2,1)S(1)}, bf16[576,512]{1,0:T(8,128)(2,1)}, u32[]{:S(2)}, u32[]{:S(2)}) collective-permute-start(bf16[576,512]{1,0:T(8,128)(2,1)S(1)} %pad_maximum_fusion.1.w0_ref), channel_id=1, source_target_pairs={{0,128},{128,256},{256,384},{384,0},{1,129},{129,257},{257,385},{3... | collective-permute-start | bytes 1769480 | tf_op jit(solution)/shard_map/weights/ppermute | solution.py:226
  73.4 13.4 %all-to-all-done.2.got_ref = bf16[16,16,640]{2,1,0:T(8,128)(2,1)} async-done(((bf16[16,16,640]{2,1,0:T(8,128)(2,1)}), bf16[16,16,640]{2,1,0:T(8,128)(2,1)}, u32[]{:S(2)}, u32[]{:S(2)}) %all-to-all-start.2) | async-done | bytes 327712 | tf_op jit(solution)/shard_map/embedded/all_to_all | solution.py:26
  86.8 1.8 embedded.1
  88.6 0.0 collective-permute-done.1.w2_ref
  88.6 0.0 collective-permute-done.w1_ref
  88.6 9.4 %all-to-all-start.3 = ((bf16[16,16,512]{2,1,0:T(8,128)(2,1)}), bf16[16,16,512]{2,1,0:T(8,128)(2,1)S(1)}, u32[]{:S(2)}, u32[]{:S(2)}) async-start(bf16[16,16,512]{2,1,0:T(8,128)(2,1)} %get-tuple-element.16), calls=%async_computation.3 | async-start | bytes 524288 | tf_op jit(solution)/shard_map/embedded/all_to_all | solution.py:26
  98.0 1.7 slice.32
  99.7 0.7 slice.33
  100.4 1.9 collective-permute-start.3
  102.3 3.9 %collective-permute-start.2 = (bf16[288,512]{1,0:T(8,128)(2,1)}, bf16[288,512]{1,0:T(8,128)(2,1)}, u32[]{:S(2)}, u32[]{:S(2)}) collective-permute-start(bf16[288,512]{1,0:T(8,128)(2,1)} %slice.32), channel_id=1, source_target_pairs={{0,128},{128,256},{256,384},{384,0},{1,129},{129,257},{257,385},{3... | collective-permute-start | bytes 884744 | tf_op jit(solution)/shard_map/embedded/ppermute | solution.py:287
  106.2 0.0 copy-done.9
  106.3 1.3 and_select_fusion
  107.6 1.7 collective-permute-done.3.w4_ref
  109.3 3.1 %collective-permute-done.2.w3_ref = bf16[288,512]{1,0:T(8,128)(2,1)} collective-permute-done((bf16[288,512]{1,0:T(8,128)(2,1)}, bf16[288,512]{1,0:T(8,128)(2,1)}, u32[]{:S(2)}, u32[]{:S(2)}) %collective-permute-start.2) | collective-permute-done | bytes 294944 | tf_op jit(solution)/shard_map/embedded/ppermute | solution.py:287
  112.4 0.0 all-to-all-done.3
  112.5 0.0 copy-done.2
  112.5 2.0 %gate_up.1 = bf16[8,32,1792]{2,1,0:T(8,128)(2,1)S(1)} custom-call(bf16[256,512]{1,0:T(8,128)(2,1)S(1)} %bitcast.35, f32[1,512]{1,0:T(1,128)S(1)} %bitcast.36, f32[1,512]{1,0:T(1,128)S(1)} %bitcast.37, bf16[576,512]{1,0:T(8,128)(2,1)S(1)} %pad_maximum_fusion.1.w0_ref, bf16[576,512]{1,0:T(8,128)(2,1)} %collective-permute-done.w1_ref, ...), custom_call_target="tpu_custom_call" | custom-call | flops 402653184 | bytes 4194304 | tf_op jit(solution)/shard_map/gate_up/pallas_call | solution.py:295
  114.5 1.0 copy-done.1
  115.5 4.6 %all-to-all-start.4 = ((bf16[8,32,1792]{2,1,0:T(8,128)(2,1)}), bf16[8,32,1792]{2,1,0:T(8,128)(2,1)}, u32[]{:S(2)}, u32[]{:S(2)}) async-start(bf16[8,32,1792]{2,1,0:T(8,128)(2,1)} %copy-done.1), calls=%async_computation.4 | async-start | bytes 1835008 | tf_op jit(solution)/shard_map/gate_up/all_to_all | solution.py:26
  120.1 0.0 copy-done.8
  120.1 0.0 copy-done.10
  120.1 0.7 fusion.7
  120.8 0.1 reshape.199
  120.9 0.1 reduce_sum.69
  121.0 0.6 dynamic_slice.9
  121.6 0.7 divide_bitcast_fusion
  122.3 12.4 %all-to-all-done.4.got_ref = bf16[8,32,1792]{2,1,0:T(8,128)(2,1)} async-done(((bf16[8,32,1792]{2,1,0:T(8,128)(2,1)}), bf16[8,32,1792]{2,1,0:T(8,128)(2,1)}, u32[]{:S(2)}, u32[]{:S(2)}) %all-to-all-start.4) | async-done | bytes 917536 | tf_op jit(solution)/shard_map/gate_up/all_to_all | solution.py:26
  134.7 0.1 broadcast_in_dim.72.weight_ref
  134.8 1.5 hidden.1
  136.3 0.1 broadcast_in_dim.74
  136.4 12.8 %all_to_all.41.got_ref = bf16[8,32,1024]{2,1,0:T(8,128)(2,1)S(1)} all-to-all(bf16[8,32,1024]{2,1,0:T(8,128)(2,1)S(1)} %broadcast_in_dim.74), channel_id=1, replica_groups=mesh['x'=4,'z'=16,'mp'=8] {'mp'}, dimensions={0} | all-to-all | bytes 1048576 | tf_op jit(solution)/shard_map/hidden/all_to_all | solution.py:26
  149.2 2.2 %down.1 = (bf16[16,16,640]{2,1,0:T(8,128)(2,1)S(1)}, f32[16,1024]{1,0:T(8,128)}) custom-call(bf16[8,32,1024]{2,1,0:T(8,128)(2,1)S(1)} %all_to_all.41.got_ref, bf16[576,512]{1,0:T(8,128)(2,1)S(1)} %pad_maximum_fusion.1.w0_ref, bf16[576,512]{1,0:T(8,128)(2,1)} %collective-permute-done.w1_ref, bf16[576,512]{1,0:T(8,128)(2,1)S(1)} %collective-permute-done.1.w2_ref, ...), custom_call_target="tpu_custom_call" | custom-call | flops 201326592 | bytes 4194304 | tf_op jit(solution)/shard_map/down/pallas_call | solution.py:345
  151.4 32.2 %all_to_all.42 = bf16[16,16,640]{2,1,0:T(8,128)(2,1)S(1)} all-to-all(bf16[16,16,640]{2,1,0:T(8,128)(2,1)S(1)} %get-tuple-element.26), channel_id=1, replica_groups=mesh['x'=4,'z'=16,'mp'=8] {'z'}, dimensions={0} | all-to-all | bytes 655360 | tf_op jit(solution)/shard_map/down/all_to_all | solution.py:26
  183.6 0.1 convert_reduce_fusion.1
  183.7 0.6 broadcast_in_dim.75
  184.4 3.2 %all-to-all-start.7 = ((f32[4,8,128]{2,1,0:T(8,128)}), f32[4,8,128]{2,1,0:T(8,128)S(1)}, u32[]{:S(2)}, u32[]{:S(2)}) async-start(f32[4,8,128]{2,1,0:T(8,128)} %broadcast_in_dim.75), calls=%async_computation.7 | async-start | bytes 32768 | tf_op jit(solution)/shard_map/results/all_to_all | solution.py:26
  187.7 0.6 add_convert_fusion
  188.3 4.7 %all-to-all-done.7 = f32[4,8,128]{2,1,0:T(8,128)S(1)} async-done(((f32[4,8,128]{2,1,0:T(8,128)}), f32[4,8,128]{2,1,0:T(8,128)S(1)}, u32[]{:S(2)}, u32[]{:S(2)}) %all-to-all-start.7) | async-done | bytes 16416 | tf_op jit(solution)/shard_map/results/all_to_all | solution.py:26
  192.9 0.1 squeeze.11
  193.0 0.6 copy.18
  (30 shorter events, 0.3 us)
Async XLA Ops:
  0.6 20.3 %copy-start = (bf16[64,128,128]{2,1,0:T(8,128)(2,1)S(1)}, bf16[64,128,128]{2,1,0:T(8,128)(2,1)}, u32[]{:S(2)}) copy-start(bf16[64,128,128]{2,1,0:T(8,128)(2,1)} %param.13) | copy-start | bytes 6291460
  2.4 37.3 %all-to-all-start = ((s32[64,8,128]{2,1,0:T(8,128)}), s32[64,8,128]{2,1,0:T(8,128)S(1)}, u32[]{:S(2)}, u32[]{:S(2)}) async-start(s32[64,8,128]{2,1,0:T(8,128)} %token_ids.1), calls=%async_computation | async-start | bytes 524288 | tf_op jit(solution)/shard_map/token_ids/all_to_all | solution.py:26
  60.5 7.0 %copy-start.3 = (bf16[192,512]{1,0:T(8,128)(2,1)S(1)}, bf16[192,512]{1,0:T(8,128)(2,1)}, u32[]{:S(2)}) copy-start(bf16[192,512]{1,0:T(8,128)(2,1)} %param.22) | copy-start | bytes 589828
  60.6 6.8 %copy-start.4 = (bf16[512,192]{0,1:T(8,128)(2,1)S(1)}, bf16[512,192]{0,1:T(8,128)(2,1)}, u32[]{:S(2)}) copy-start(bf16[512,192]{0,1:T(8,128)(2,1)} %param.21) | copy-start | bytes 589828
  60.6 6.8 %copy-start.5 = (bf16[512,192]{0,1:T(8,128)(2,1)S(1)}, bf16[512,192]{0,1:T(8,128)(2,1)}, u32[]{:S(2)}) copy-start(bf16[512,192]{0,1:T(8,128)(2,1)} %param.20) | copy-start | bytes 589828
  61.4 25.4 %all-to-all-start.2 = ((bf16[16,16,640]{2,1,0:T(8,128)(2,1)}), bf16[16,16,640]{2,1,0:T(8,128)(2,1)}, u32[]{:S(2)}, u32[]{:S(2)}) async-start(bf16[16,16,640]{2,1,0:T(8,128)(2,1)} %pad_maximum_fusion.2), calls=%async_computation.2 | async-start | bytes 655360 | tf_op jit(solution)/shard_map/embedded/all_to_all | solution.py:26
  67.5 38.8 %copy-start.9 = (bf16[512]{0:T(512)(128)(2,1)S(1)}, bf16[512]{0:T(512)(128)(2,1)}, u32[]{:S(2)}) copy-start(bf16[512]{0:T(512)(128)(2,1)} %param.19) | copy-start | bytes 3076
  67.5 45.0 %copy-start.2 = (f32[512]{0:T(512)S(1)}, f32[512]{0:T(512)}, u32[]{:S(2)}) copy-start(f32[512]{0:T(512)} %param.23) | copy-start | bytes 6148
  67.5 21.1 %collective-permute-start.1 = (bf16[576,512]{1,0:T(8,128)(2,1)S(1)}, bf16[576,512]{1,0:T(8,128)(2,1)S(1)}, u32[]{:S(2)}, u32[]{:S(2)}) collective-permute-start(bf16[576,512]{1,0:T(8,128)(2,1)S(1)} %pad_maximum_fusion.1.w0_ref), channel_id=1, source_target_pairs={{0,384},{128,0},{256,128},{384,256},{1,385},{129,1},{257,129},{385... | collective-permute-start | bytes 1769480 | tf_op jit(solution)/shard_map/weights/ppermute | solution.py:226
  70.6 18.0 %collective-permute-start = (bf16[576,512]{1,0:T(8,128)(2,1)S(1)}, bf16[576,512]{1,0:T(8,128)(2,1)}, u32[]{:S(2)}, u32[]{:S(2)}) collective-permute-start(bf16[576,512]{1,0:T(8,128)(2,1)S(1)} %pad_maximum_fusion.1.w0_ref), channel_id=1, source_target_pairs={{0,128},{128,256},{256,384},{384,0},{1,129},{129,257},{257,385},{3... | collective-permute-start | bytes 1769480 | tf_op jit(solution)/shard_map/weights/ppermute | solution.py:226
  88.6 23.8 %all-to-all-start.3 = ((bf16[16,16,512]{2,1,0:T(8,128)(2,1)}), bf16[16,16,512]{2,1,0:T(8,128)(2,1)S(1)}, u32[]{:S(2)}, u32[]{:S(2)}) async-start(bf16[16,16,512]{2,1,0:T(8,128)(2,1)} %get-tuple-element.16), calls=%async_computation.3 | async-start | bytes 524288 | tf_op jit(solution)/shard_map/embedded/all_to_all | solution.py:26
  100.4 8.9 %collective-permute-start.3 = (bf16[288,512]{1,0:T(8,128)(2,1)}, bf16[288,512]{1,0:T(8,128)(2,1)}, u32[]{:S(2)}, u32[]{:S(2)}) collective-permute-start(bf16[288,512]{1,0:T(8,128)(2,1)} %slice.33), channel_id=1, source_target_pairs={{0,384},{128,0},{256,128},{384,256},{1,385},{129,1},{257,129},{385... | collective-permute-start | bytes 884744 | tf_op jit(solution)/shard_map/embedded/ppermute | solution.py:288
  102.3 10.1 %collective-permute-start.2 = (bf16[288,512]{1,0:T(8,128)(2,1)}, bf16[288,512]{1,0:T(8,128)(2,1)}, u32[]{:S(2)}, u32[]{:S(2)}) collective-permute-start(bf16[288,512]{1,0:T(8,128)(2,1)} %slice.32), channel_id=1, source_target_pairs={{0,128},{128,256},{256,384},{384,0},{1,129},{129,257},{257,385},{3... | collective-permute-start | bytes 884744 | tf_op jit(solution)/shard_map/embedded/ppermute | solution.py:287
  114.5 1.0 copy-start.1
  115.4 4.6 %copy-start.7 = (s32[2,1024]{1,0:T(2,128)S(1)}, s32[2,1024]{1,0:T(2,128)}, u32[]{:S(2)}) copy-start(s32[2,1024]{1,0:T(2,128)} %get-tuple-element.39) | copy-start | bytes 24580
  115.4 4.6 %copy-start.8 = (s32[2,1024]{1,0:T(2,128)S(1)}, s32[2,1024]{1,0:T(2,128)}, u32[]{:S(2)}) copy-start(s32[2,1024]{1,0:T(2,128)} %get-tuple-element.40) | copy-start | bytes 24580
  115.4 4.6 %copy-start.10 = (f32[2,32,128]{2,1,0:T(8,128)S(1)}, f32[2,32,128]{2,1,0:T(8,128)}, u32[]{:S(2)}) copy-start(f32[2,32,128]{2,1,0:T(8,128)} %get-tuple-element.23) | copy-start | bytes 98308
  115.5 19.3 %all-to-all-start.4 = ((bf16[8,32,1792]{2,1,0:T(8,128)(2,1)}), bf16[8,32,1792]{2,1,0:T(8,128)(2,1)}, u32[]{:S(2)}, u32[]{:S(2)}) async-start(bf16[8,32,1792]{2,1,0:T(8,128)(2,1)} %copy-done.1), calls=%async_computation.4 | async-start | bytes 1835008 | tf_op jit(solution)/shard_map/gate_up/all_to_all | solution.py:26
  149.2 38.4 %copy-start.6 = (f32[16,512]{1,0:T(8,128)S(1)}, f32[16,512]{1,0:T(8,128)}, u32[]{:S(2)}) copy-start(f32[16,512]{1,0:T(8,128)} %get-tuple-element.25) | copy-start | bytes 98308
  184.4 8.6 %all-to-all-start.7 = ((f32[4,8,128]{2,1,0:T(8,128)}), f32[4,8,128]{2,1,0:T(8,128)S(1)}, u32[]{:S(2)}, u32[]{:S(2)}) async-start(f32[4,8,128]{2,1,0:T(8,128)} %broadcast_in_dim.75), calls=%async_computation.7 | async-start | bytes 32768 | tf_op jit(solution)/shard_map/results/all_to_all | solution.py:26

commit v4 on v3

--- a/solution.py
+++ b/solution.py
@@ -231,7 +231,7 @@
         base = (corpus_index * pass_count).astype(jnp.int32).reshape(1)
         coded = pl.pallas_call(
             ids_kernel,
-            out_shape=jax.ShapeDtypeStruct((NX * NZ, tokens // LANES, LANES), jnp.int32),
+            out_shape=jax.ShapeDtypeStruct((NZ, tokens // LANES, LANES), jnp.int32),
             in_specs=[smem] * 3 + [vmem],
             out_specs=vmem,
             scratch_shapes=[
@@ -239,8 +239,8 @@
                 pltpu.VMEM((tokens // LANES, LANES), jnp.int32),
             ],
         )(base, retained_documents.T, document_extent, document_vocab_codes.T)
-        coded = swap(coded, CORPUS)
-        coded = jnp.sum(coded, axis=0).reshape(tokens)
+        coded = jnp.sum(swap(coded, "z"), axis=0)
+        coded = jnp.sum(share_with(coded, "x", NX), axis=0).reshape(tokens)
         token_ids = coded // 2
 
     with jax.named_scope("passage_scores"):

time: 195 us -> 188 us (0.964)
  waiting for transfers between devices: 52.2 us -> 45.7 us
  starting transfers between devices: 52.6 us -> 55.2 us
  blocking collectives: 62.6 us -> 60.4 us
    all_to_all x5 -> x6, waiting for transfers between devices: 47.4 us -> 40.8 us  [swap(): return lax.all_to_all(v, axis, 0, 0, tiled=True)]
    all_to_all x5 -> x6, starting transfers between devices: 41 us -> 43.5 us  [swap(): return lax.all_to_all(v, axis, 0, 0, tiled=True)]
    all_to_all x3, blocking collectives: 62.6 us -> 60.4 us  [swap(): return lax.all_to_all(v, axis, 0, 0, tiled=True)]
  transfers between devices with their start and end apart: 9 -> 10, of which waited for: 6 -> 7; matrix products, arithmetic and copies ran while one was open for 5% -> 5% of each run, Pallas kernels for 1% -> 1%
where the time goes in v4:
time: 188 us; the launch traced here: 187 us
  blocking collectives  60.4 us (32%)
  starting transfers between devices  55.2 us (29%)
  waiting for transfers between devices  45.7 us (24%)
  Pallas kernels  9.23 us (5%)
  local copies, waits for them, and re-layouts  6.36 us (3%)
  other arithmetic  4.83 us (3%)
  matrix products  4.03 us (2%)
    all_to_all x3, blocking collectives, swap(): return lax.all_to_all(v, axis, 0, 0, tiled=True)  60.4 us
    all_to_all x6, starting transfers between devices, swap(): return lax.all_to_all(v, axis, 0, 0, tiled=True)  43.5 us
    all_to_all x6, waiting for transfers between devices, swap(): return lax.all_to_all(v, axis, 0, 0, tiled=True)  40.8 us
    ppermute x1, starting transfers between devices, body(): weights.append(lax.ppermute(weights[1][:middle], 'x', up))  3.92 us
  transfers between devices with their start and end apart: 10, of which 7 were waited for; matrix products, arithmetic and copies ran while one was open for 5% of the time, Pallas kernels for 1%

profile of v4, /device:TPU:64, one launch (start us, length us, event | category | flops | bytes accessed | tf_op | source)
XLA Modules:
  0.0 186.7 jit_solution(5562763878385625015)
XLA Ops:
  0.6 0.0 copy-start
  0.7 1.7 token_ids.1
  2.3 14.8 %all-to-all-start = ((s32[16,8,128]{2,1,0:T(8,128)}), s32[16,8,128]{2,1,0:T(8,128)S(1)}, u32[]{:S(2)}, u32[]{:S(2)}) async-start(s32[16,8,128]{2,1,0:T(8,128)} %token_ids.1), calls=%async_computation | async-start | bytes 131072 | tf_op jit(solution)/shard_map/token_ids/all_to_all | solution.py:26
  17.1 0.7 iota_compare_fusion.7
  17.8 0.0 copy-done
  17.8 0.0 copy-start.10
  17.8 1.8 select_reduce_fusion
  19.6 0.1 reduce_sum.77
  19.7 0.1 reshape.197
  19.8 8.4 %all-to-all-done = s32[16,8,128]{2,1,0:T(8,128)S(1)} async-done(((s32[16,8,128]{2,1,0:T(8,128)}), s32[16,8,128]{2,1,0:T(8,128)S(1)}, u32[]{:S(2)}, u32[]{:S(2)}) %all-to-all-start) | async-done | bytes 65568 | tf_op jit(solution)/shard_map/token_ids/all_to_all | solution.py:26
  28.2 0.6 broadcast_in_dim.36
  28.8 4.3 %all-to-all-start.1 = ((s32[4,8,128]{2,1,0:T(8,128)}), s32[4,8,128]{2,1,0:T(8,128)S(1)}, u32[]{:S(2)}, u32[]{:S(2)}) async-start(s32[4,8,128]{2,1,0:T(8,128)} %broadcast_in_dim.36), calls=%async_computation.1 | async-start | bytes 32768 | tf_op jit(solution)/shard_map/token_ids/all_to_all | solution.py:26
  33.1 5.3 %all-to-all-done.1 = s32[4,8,128]{2,1,0:T(8,128)S(1)} async-done(((s32[4,8,128]{2,1,0:T(8,128)}), s32[4,8,128]{2,1,0:T(8,128)S(1)}, u32[]{:S(2)}, u32[]{:S(2)}) %all-to-all-start.1) | async-done | bytes 16416 | tf_op jit(solution)/shard_map/token_ids/all_to_all | solution.py:26
  38.5 0.0 copy-done.10
  38.5 1.6 fusion.6
  40.0 0.1 pad_maximum_fusion
  40.1 15.4 %all_to_all.45 = bf16[4,264,512]{2,1,0:T(8,128)(2,1)S(1)} all-to-all(bf16[4,264,512]{2,1,0:T(8,128)(2,1)S(1)} %pad_maximum_fusion), channel_id=1, replica_groups=mesh['x'=4,'z'=16,'mp'=8] {'x'}, dimensions={0} | all-to-all | bytes 2162688 | tf_op jit(solution)/shard_map/embedded/all_to_all | solution.py:26
  55.6 0.0 copy-start.3
  55.6 0.1 slice_reduce_fusion
  55.7 0.0 copy-start.4
  55.7 0.0 copy-start.5
  55.8 0.8 pad_maximum_fusion.2
  56.5 5.6 %all-to-all-start.3 = ((bf16[16,16,640]{2,1,0:T(8,128)(2,1)}), bf16[16,16,640]{2,1,0:T(8,128)(2,1)}, u32[]{:S(2)}, u32[]{:S(2)}) async-start(bf16[16,16,640]{2,1,0:T(8,128)(2,1)} %pad_maximum_fusion.2), calls=%async_computation.3 | async-start | bytes 655360 | tf_op jit(solution)/shard_map/embedded/all_to_all | solution.py:26
  62.2 0.0 copy-start.9
  62.2 0.0 copy-start.2
  62.2 3.1 %collective-permute-start.1 = (bf16[576,512]{1,0:T(8,128)(2,1)S(1)}, bf16[576,512]{1,0:T(8,128)(2,1)S(1)}, u32[]{:S(2)}, u32[]{:S(2)}) collective-permute-start(bf16[576,512]{1,0:T(8,128)(2,1)S(1)} %pad_maximum_fusion.1.w0_ref), channel_id=1, source_target_pairs={{0,384},{128,0},{256,128},{384,256},{1,385},{129,1},{257,129},{385... | collective-permute-start | bytes 1769480 | tf_op jit(solution)/shard_map/weights/ppermute | solution.py:226
  65.3 2.8 %collective-permute-start = (bf16[576,512]{1,0:T(8,128)(2,1)S(1)}, bf16[576,512]{1,0:T(8,128)(2,1)}, u32[]{:S(2)}, u32[]{:S(2)}) collective-permute-start(bf16[576,512]{1,0:T(8,128)(2,1)S(1)} %pad_maximum_fusion.1.w0_ref), channel_id=1, source_target_pairs={{0,128},{128,256},{256,384},{384,0},{1,129},{129,257},{257,385},{3... | collective-permute-start | bytes 1769480 | tf_op jit(solution)/shard_map/weights/ppermute | solution.py:226
  68.0 10.1 %all-to-all-done.3.got_ref = bf16[16,16,640]{2,1,0:T(8,128)(2,1)} async-done(((bf16[16,16,640]{2,1,0:T(8,128)(2,1)}), bf16[16,16,640]{2,1,0:T(8,128)(2,1)}, u32[]{:S(2)}, u32[]{:S(2)}) %all-to-all-start.3) | async-done | bytes 327712 | tf_op jit(solution)/shard_map/embedded/all_to_all | solution.py:26
  78.1 1.8 embedded.1
  79.9 0.0 collective-permute-done.1.w2_ref
  79.9 0.0 collective-permute-done.w1_ref
  79.9 11.0 %all-to-all-start.4 = ((bf16[16,16,512]{2,1,0:T(8,128)(2,1)}), bf16[16,16,512]{2,1,0:T(8,128)(2,1)S(1)}, u32[]{:S(2)}, u32[]{:S(2)}) async-start(bf16[16,16,512]{2,1,0:T(8,128)(2,1)} %get-tuple-element.16), calls=%async_computation.4 | async-start | bytes 524288 | tf_op jit(solution)/shard_map/embedded/all_to_all | solution.py:26
  91.0 1.7 slice.32
  92.7 0.7 slice.33
  93.4 1.9 %collective-permute-start.3 = (bf16[288,512]{1,0:T(8,128)(2,1)}, bf16[288,512]{1,0:T(8,128)(2,1)}, u32[]{:S(2)}, u32[]{:S(2)}) collective-permute-start(bf16[288,512]{1,0:T(8,128)(2,1)} %slice.33), channel_id=1, source_target_pairs={{0,384},{128,0},{256,128},{384,256},{1,385},{129,1},{257,129},{385... | collective-permute-start | bytes 884744 | tf_op jit(solution)/shard_map/embedded/ppermute | solution.py:288
  95.3 3.9 %collective-permute-start.2 = (bf16[288,512]{1,0:T(8,128)(2,1)}, bf16[288,512]{1,0:T(8,128)(2,1)}, u32[]{:S(2)}, u32[]{:S(2)}) collective-permute-start(bf16[288,512]{1,0:T(8,128)(2,1)} %slice.32), channel_id=1, source_target_pairs={{0,128},{128,256},{256,384},{384,0},{1,129},{129,257},{257,385},{3... | collective-permute-start | bytes 884744 | tf_op jit(solution)/shard_map/embedded/ppermute | solution.py:287
  99.3 1.3 and_select_fusion
  100.6 1.7 collective-permute-done.3.w4_ref
  102.3 3.1 %collective-permute-done.2.w3_ref = bf16[288,512]{1,0:T(8,128)(2,1)} collective-permute-done((bf16[288,512]{1,0:T(8,128)(2,1)}, bf16[288,512]{1,0:T(8,128)(2,1)}, u32[]{:S(2)}, u32[]{:S(2)}) %collective-permute-start.2) | collective-permute-done | bytes 294944 | tf_op jit(solution)/shard_map/embedded/ppermute | solution.py:287
  105.5 0.0 all-to-all-done.4
  105.5 2.0 %gate_up.1 = bf16[8,32,1792]{2,1,0:T(8,128)(2,1)S(1)} custom-call(bf16[256,512]{1,0:T(8,128)(2,1)S(1)} %bitcast.35, f32[1,512]{1,0:T(1,128)S(1)} %bitcast.36, f32[1,512]{1,0:T(1,128)S(1)} %bitcast.37, bf16[576,512]{1,0:T(8,128)(2,1)S(1)} %pad_maximum_fusion.1.w0_ref, bf16[576,512]{1,0:T(8,128)(2,1)} %collective-permute-done.w1_ref, ...), custom_call_target="tpu_custom_call" | custom-call | flops 402653184 | bytes 4194304 | tf_op jit(solution)/shard_map/gate_up/pallas_call | solution.py:295
  107.5 1.0 copy-done.1
  108.5 4.6 %all-to-all-start.5 = ((bf16[8,32,1792]{2,1,0:T(8,128)(2,1)}), bf16[8,32,1792]{2,1,0:T(8,128)(2,1)}, u32[]{:S(2)}, u32[]{:S(2)}) async-start(bf16[8,32,1792]{2,1,0:T(8,128)(2,1)} %copy-done.1), calls=%async_computation.5 | async-start | bytes 1835008 | tf_op jit(solution)/shard_map/gate_up/all_to_all | solution.py:26
  113.1 0.0 copy-done.8
  113.1 0.0 copy-done.11
  113.1 0.7 fusion.7
  113.8 0.1 reshape.200
  113.9 0.1 reduce_sum.79
  114.0 0.6 dynamic_slice.9
  114.6 0.7 divide_bitcast_fusion
  115.3 12.4 %all-to-all-done.5.got_ref = bf16[8,32,1792]{2,1,0:T(8,128)(2,1)} async-done(((bf16[8,32,1792]{2,1,0:T(8,128)(2,1)}), bf16[8,32,1792]{2,1,0:T(8,128)(2,1)}, u32[]{:S(2)}, u32[]{:S(2)}) %all-to-all-start.5) | async-done | bytes 917536 | tf_op jit(solution)/shard_map/gate_up/all_to_all | solution.py:26
  127.7 0.1 broadcast_in_dim.79.weight_ref
  127.8 1.5 hidden.1
  129.3 0.1 broadcast_in_dim.81
  129.4 12.8 %all_to_all.46.got_ref = bf16[8,32,1024]{2,1,0:T(8,128)(2,1)S(1)} all-to-all(bf16[8,32,1024]{2,1,0:T(8,128)(2,1)S(1)} %broadcast_in_dim.81), channel_id=1, replica_groups=mesh['x'=4,'z'=16,'mp'=8] {'mp'}, dimensions={0} | all-to-all | bytes 1048576 | tf_op jit(solution)/shard_map/hidden/all_to_all | solution.py:26
  142.2 2.2 %down.1 = (bf16[16,16,640]{2,1,0:T(8,128)(2,1)S(1)}, f32[16,1024]{1,0:T(8,128)}) custom-call(bf16[8,32,1024]{2,1,0:T(8,128)(2,1)S(1)} %all_to_all.46.got_ref, bf16[576,512]{1,0:T(8,128)(2,1)S(1)} %pad_maximum_fusion.1.w0_ref, bf16[576,512]{1,0:T(8,128)(2,1)} %collective-permute-done.w1_ref, bf16[576,512]{1,0:T(8,128)(2,1)S(1)} %collective-permute-done.1.w2_ref, ...), custom_call_target="tpu_custom_call" | custom-call | flops 201326592 | bytes 4194304 | tf_op jit(solution)/shard_map/down/pallas_call | solution.py:345
  144.4 32.2 %all_to_all.47 = bf16[16,16,640]{2,1,0:T(8,128)(2,1)S(1)} all-to-all(bf16[16,16,640]{2,1,0:T(8,128)(2,1)S(1)} %get-tuple-element.26), channel_id=1, replica_groups=mesh['x'=4,'z'=16,'mp'=8] {'z'}, dimensions={0} | all-to-all | bytes 655360 | tf_op jit(solution)/shard_map/down/all_to_all | solution.py:26
  176.6 0.1 convert_reduce_fusion.1
  176.7 0.6 broadcast_in_dim.82
  177.4 3.2 %all-to-all-start.8 = ((f32[4,8,128]{2,1,0:T(8,128)}), f32[4,8,128]{2,1,0:T(8,128)S(1)}, u32[]{:S(2)}, u32[]{:S(2)}) async-start(f32[4,8,128]{2,1,0:T(8,128)} %broadcast_in_dim.82), calls=%async_computation.8 | async-start | bytes 32768 | tf_op jit(solution)/shard_map/results/all_to_all | solution.py:26
  180.7 0.6 add_convert_fusion
  181.3 4.7 %all-to-all-done.8 = f32[4,8,128]{2,1,0:T(8,128)S(1)} async-done(((f32[4,8,128]{2,1,0:T(8,128)}), f32[4,8,128]{2,1,0:T(8,128)S(1)}, u32[]{:S(2)}, u32[]{:S(2)}) %all-to-all-start.8) | async-done | bytes 16416 | tf_op jit(solution)/shard_map/results/all_to_all | solution.py:26
  185.9 0.1 squeeze.11
  186.0 0.6 copy.19
  (36 shorter events, 0.3 us)
Async XLA Ops:
  0.6 17.2 %copy-start = (bf16[64,128,128]{2,1,0:T(8,128)(2,1)S(1)}, bf16[64,128,128]{2,1,0:T(8,128)(2,1)}, u32[]{:S(2)}) copy-start(bf16[64,128,128]{2,1,0:T(8,128)(2,1)} %param.13) | copy-start | bytes 6291460
  2.3 25.8 %all-to-all-start = ((s32[16,8,128]{2,1,0:T(8,128)}), s32[16,8,128]{2,1,0:T(8,128)S(1)}, u32[]{:S(2)}, u32[]{:S(2)}) async-start(s32[16,8,128]{2,1,0:T(8,128)} %token_ids.1), calls=%async_computation | async-start | bytes 131072 | tf_op jit(solution)/shard_map/token_ids/all_to_all | solution.py:26
  17.8 20.6 %copy-start.10 = (bf16[1200,512]{1,0:T(8,128)(2,1)S(1)}, bf16[1200,512]{1,0:T(8,128)(2,1)}, u32[]{:S(2)}) copy-start(bf16[1200,512]{1,0:T(8,128)(2,1)} %param.18) | copy-start | bytes 3686404
  28.8 9.7 %all-to-all-start.1 = ((s32[4,8,128]{2,1,0:T(8,128)}), s32[4,8,128]{2,1,0:T(8,128)S(1)}, u32[]{:S(2)}, u32[]{:S(2)}) async-start(s32[4,8,128]{2,1,0:T(8,128)} %broadcast_in_dim.36), calls=%async_computation.1 | async-start | bytes 32768 | tf_op jit(solution)/shard_map/token_ids/all_to_all | solution.py:26
  55.6 6.5 %copy-start.3 = (bf16[192,512]{1,0:T(8,128)(2,1)S(1)}, bf16[192,512]{1,0:T(8,128)(2,1)}, u32[]{:S(2)}) copy-start(bf16[192,512]{1,0:T(8,128)(2,1)} %param.22) | copy-start | bytes 589828
  55.7 6.4 %copy-start.4 = (bf16[512,192]{0,1:T(8,128)(2,1)S(1)}, bf16[512,192]{0,1:T(8,128)(2,1)}, u32[]{:S(2)}) copy-start(bf16[512,192]{0,1:T(8,128)(2,1)} %param.21) | copy-start | bytes 589828
  55.7 6.4 %copy-start.5 = (bf16[512,192]{0,1:T(8,128)(2,1)S(1)}, bf16[512,192]{0,1:T(8,128)(2,1)}, u32[]{:S(2)}) copy-start(bf16[512,192]{0,1:T(8,128)(2,1)} %param.20) | copy-start | bytes 589828
  56.5 21.6 %all-to-all-start.3 = ((bf16[16,16,640]{2,1,0:T(8,128)(2,1)}), bf16[16,16,640]{2,1,0:T(8,128)(2,1)}, u32[]{:S(2)}, u32[]{:S(2)}) async-start(bf16[16,16,640]{2,1,0:T(8,128)(2,1)} %pad_maximum_fusion.2), calls=%async_computation.3 | async-start | bytes 655360 | tf_op jit(solution)/shard_map/embedded/all_to_all | solution.py:26
  62.2 37.1 %copy-start.9 = (bf16[512]{0:T(512)(128)(2,1)S(1)}, bf16[512]{0:T(512)(128)(2,1)}, u32[]{:S(2)}) copy-start(bf16[512]{0:T(512)(128)(2,1)} %param.19) | copy-start | bytes 3076
  62.2 43.3 %copy-start.2 = (f32[512]{0:T(512)S(1)}, f32[512]{0:T(512)}, u32[]{:S(2)}) copy-start(f32[512]{0:T(512)} %param.23) | copy-start | bytes 6148
  62.2 17.8 %collective-permute-start.1 = (bf16[576,512]{1,0:T(8,128)(2,1)S(1)}, bf16[576,512]{1,0:T(8,128)(2,1)S(1)}, u32[]{:S(2)}, u32[]{:S(2)}) collective-permute-start(bf16[576,512]{1,0:T(8,128)(2,1)S(1)} %pad_maximum_fusion.1.w0_ref), channel_id=1, source_target_pairs={{0,384},{128,0},{256,128},{384,256},{1,385},{129,1},{257,129},{385... | collective-permute-start | bytes 1769480 | tf_op jit(solution)/shard_map/weights/ppermute | solution.py:226
  65.3 14.7 %collective-permute-start = (bf16[576,512]{1,0:T(8,128)(2,1)S(1)}, bf16[576,512]{1,0:T(8,128)(2,1)}, u32[]{:S(2)}, u32[]{:S(2)}) collective-permute-start(bf16[576,512]{1,0:T(8,128)(2,1)S(1)} %pad_maximum_fusion.1.w0_ref), channel_id=1, source_target_pairs={{0,128},{128,256},{256,384},{384,0},{1,129},{129,257},{257,385},{3... | collective-permute-start | bytes 1769480 | tf_op jit(solution)/shard_map/weights/ppermute | solution.py:226
  79.9 25.5 %all-to-all-start.4 = ((bf16[16,16,512]{2,1,0:T(8,128)(2,1)}), bf16[16,16,512]{2,1,0:T(8,128)(2,1)S(1)}, u32[]{:S(2)}, u32[]{:S(2)}) async-start(bf16[16,16,512]{2,1,0:T(8,128)(2,1)} %get-tuple-element.16), calls=%async_computation.4 | async-start | bytes 524288 | tf_op jit(solution)/shard_map/embedded/all_to_all | solution.py:26
  93.4 8.9 %collective-permute-start.3 = (bf16[288,512]{1,0:T(8,128)(2,1)}, bf16[288,512]{1,0:T(8,128)(2,1)}, u32[]{:S(2)}, u32[]{:S(2)}) collective-permute-start(bf16[288,512]{1,0:T(8,128)(2,1)} %slice.33), channel_id=1, source_target_pairs={{0,384},{128,0},{256,128},{384,256},{1,385},{129,1},{257,129},{385... | collective-permute-start | bytes 884744 | tf_op jit(solution)/shard_map/embedded/ppermute | solution.py:288
  95.3 10.1 %collective-permute-start.2 = (bf16[288,512]{1,0:T(8,128)(2,1)}, bf16[288,512]{1,0:T(8,128)(2,1)}, u32[]{:S(2)}, u32[]{:S(2)}) collective-permute-start(bf16[288,512]{1,0:T(8,128)(2,1)} %slice.32), channel_id=1, source_target_pairs={{0,128},{128,256},{256,384},{384,0},{1,129},{129,257},{257,385},{3... | collective-permute-start | bytes 884744 | tf_op jit(solution)/shard_map/embedded/ppermute | solution.py:287
  107.5 1.0 copy-start.1
  108.4 4.6 %copy-start.7 = (s32[2,1024]{1,0:T(2,128)S(1)}, s32[2,1024]{1,0:T(2,128)}, u32[]{:S(2)}) copy-start(s32[2,1024]{1,0:T(2,128)} %get-tuple-element.42) | copy-start | bytes 24580
  108.4 4.6 %copy-start.8 = (s32[2,1024]{1,0:T(2,128)S(1)}, s32[2,1024]{1,0:T(2,128)}, u32[]{:S(2)}) copy-start(s32[2,1024]{1,0:T(2,128)} %get-tuple-element.43) | copy-start | bytes 24580
  108.4 4.6 %copy-start.11 = (f32[2,32,128]{2,1,0:T(8,128)S(1)}, f32[2,32,128]{2,1,0:T(8,128)}, u32[]{:S(2)}) copy-start(f32[2,32,128]{2,1,0:T(8,128)} %get-tuple-element.23) | copy-start | bytes 98308
  108.5 19.3 %all-to-all-start.5 = ((bf16[8,32,1792]{2,1,0:T(8,128)(2,1)}), bf16[8,32,1792]{2,1,0:T(8,128)(2,1)}, u32[]{:S(2)}, u32[]{:S(2)}) async-start(bf16[8,32,1792]{2,1,0:T(8,128)(2,1)} %copy-done.1), calls=%async_computation.5 | async-start | bytes 1835008 | tf_op jit(solution)/shard_map/gate_up/all_to_all | solution.py:26
  142.2 38.4 %copy-start.6 = (f32[16,512]{1,0:T(8,128)S(1)}, f32[16,512]{1,0:T(8,128)}, u32[]{:S(2)}) copy-start(f32[16,512]{1,0:T(8,128)} %get-tuple-element.25) | copy-start | bytes 98308
  177.4 8.6 %all-to-all-start.8 = ((f32[4,8,128]{2,1,0:T(8,128)}), f32[4,8,128]{2,1,0:T(8,128)S(1)}, u32[]{:S(2)}, u32[]{:S(2)}) async-start(f32[4,8,128]{2,1,0:T(8,128)} %broadcast_in_dim.82), calls=%async_computation.8 | async-start | bytes 32768 | tf_op jit(solution)/shard_map/results/all_to_all | solution.py:26

commit v5 on v4

--- a/solution.py
+++ b/solution.py
@@ -183,10 +183,13 @@
             [picks[i * lines // picks.shape[1], at + j : at + j + 1] for j in range(lines)], axis=1
         )
     rider = fill((n_mp, LANES), 1, (shares[:, 0], shares[:, 1], shares[:, 2]))
-    rider = jnp.concatenate([rider, jnp.zeros((share - n_mp, LANES), F32)], axis=0).astype(BF16)
+    rider = rider.astype(BF16)
     for target in range(groups):
-        out_ref[target, :, : down.shape[1]] = down[target * share : (target + 1) * share].astype(BF16)
-        out_ref[target, :, down.shape[1] :] = rider
+        block = down[target * share : (target + 1) * share].astype(BF16)
+        for part in range(down.shape[1] // LANES):
+            rows = slice(part * share, (part + 1) * share)
+            out_ref[target, rows, :] = block[:, part * LANES : (part + 1) * LANES]
+        out_ref[target, out_ref.shape[1] - n_mp :, :] = rider
 
 
 def body(
@@ -240,7 +243,7 @@
             ],
         )(base, retained_documents.T, document_extent, document_vocab_codes.T)
         coded = jnp.sum(swap(coded, "z"), axis=0)
-        coded = jnp.sum(share_with(coded, "x", NX), axis=0).reshape(tokens)
+        coded = lax.psum(coded, "x").reshape(tokens)
         token_ids = coded // 2
 
     with jax.named_scope("passage_scores"):
@@ -345,7 +348,7 @@
         sent, shortlist_maxsim = pl.pallas_call(
             functools.partial(down_kernel, n_mp, units, half),
             out_shape=(
-                jax.ShapeDtypeStruct((NZ, share, width + LANES), BF16),
+                jax.ShapeDtypeStruct((NZ, share * width // LANES + n_mp, LANES), BF16),
                 jax.ShapeDtypeStruct((n_mp * query_count, shortlist_documents.shape[1]), F32),
             ),
             in_specs=[vmem] * 6,
@@ -357,11 +360,12 @@
             ),
         )(hidden, *weights)
         got = swap(sent, "z")
-        total = own + jnp.sum(got[:, :, :width].astype(F32), axis=0)
+        total = jnp.sum(got[:, :-n_mp].astype(F32), axis=0).reshape(-1, share, LANES)
+        total = own + jnp.transpose(total, (1, 0, 2)).reshape(share, width)
         layer_result = total.astype(BF16)
 
     with jax.named_scope("results"):
-        merit = jnp.sum(got[:, :n_mp, width : width + 3].astype(F32), axis=(0, 2))
+        merit = jnp.sum(got[:, -n_mp:, :3].astype(F32), axis=(0, 2))
         merit = jnp.broadcast_to(jnp.pad(merit, (0, LANES - n_mp))[None], (8, LANES))
         merit = share_with(merit, "x", NX)[:, 0, :n_mp]
 

time: 188 us -> 184 us (0.979)
  blocking collectives: 60.4 us -> 67.5 us
  waiting for transfers between devices: 45.7 us -> 40.3 us
  starting transfers between devices: 55.2 us -> 50.6 us
    psum x0 -> x1, blocking collectives: none -> 8.91 us  [body(): coded = lax.psum(coded, 'x').reshape(tokens)]
    all_to_all x6 -> x5, waiting for transfers between devices: 40.8 us -> 35.4 us  [swap(): return lax.all_to_all(v, axis, 0, 0, tiled=True)]
    all_to_all x6 -> x5, starting transfers between devices: 43.5 us -> 38.9 us  [swap(): return lax.all_to_all(v, axis, 0, 0, tiled=True)]
  transfers between devices with their start and end apart: 10 -> 9, of which waited for: 7 -> 6; matrix products, arithmetic and copies ran while one was open for 5% -> 5% of each run, Pallas kernels for 1% -> 1%
where the time goes in v5:
time: 184 us; the launch traced here: 183 us
  blocking collectives  67.5 us (37%)
  starting transfers between devices  50.6 us (28%)
  waiting for transfers between devices  40.3 us (22%)
  Pallas kernels  9.22 us (5%)
  local copies, waits for them, and re-layouts  5.74 us (3%)
  other arithmetic  4.82 us (3%)
  matrix products  4.03 us (2%)
    all_to_all x3, blocking collectives, swap(): return lax.all_to_all(v, axis, 0, 0, tiled=True)  58.6 us
    all_to_all x5, starting transfers between devices, swap(): return lax.all_to_all(v, axis, 0, 0, tiled=True)  38.9 us
    all_to_all x5, waiting for transfers between devices, swap(): return lax.all_to_all(v, axis, 0, 0, tiled=True)  35.4 us
    psum x1, blocking collectives, body(): coded = lax.psum(coded, 'x').reshape(tokens)  8.91 us
    ppermute x1, starting transfers between devices, body(): weights.append(lax.ppermute(weights[1][:middle], 'x', up))  3.92 us
  transfers between devices with their start and end apart: 9, of which 6 were waited for; matrix products, arithmetic and copies ran while one was open for 5% of the time, Pallas kernels for 1%

profile of v5, /device:TPU:64, one launch (start us, length us, event | category | flops | bytes accessed | tf_op | source)
XLA Modules:
  0.0 183.2 jit_solution(3215335416527347423)
XLA Ops:
  0.6 0.0 copy-start
  0.7 1.7 token_ids.1
  2.3 14.8 %all-to-all-start = ((s32[16,8,128]{2,1,0:T(8,128)}), s32[16,8,128]{2,1,0:T(8,128)S(1)}, u32[]{:S(2)}, u32[]{:S(2)}) async-start(s32[16,8,128]{2,1,0:T(8,128)} %token_ids.1), calls=%async_computation | async-start | bytes 131072 | tf_op jit(solution)/shard_map/token_ids/all_to_all | solution.py:26
  17.1 0.7 iota_compare_fusion.7
  17.8 0.0 copy-done
  17.8 0.0 copy-start.10
  17.8 1.8 select_reduce_fusion
  19.6 0.1 reduce_sum.67
  19.7 0.1 reshape.202
  19.8 8.3 %all-to-all-done = s32[16,8,128]{2,1,0:T(8,128)S(1)} async-done(((s32[16,8,128]{2,1,0:T(8,128)}), s32[16,8,128]{2,1,0:T(8,128)S(1)}, u32[]{:S(2)}, u32[]{:S(2)}) %all-to-all-start) | async-done | bytes 65568 | tf_op jit(solution)/shard_map/token_ids/all_to_all | solution.py:26
  28.2 8.9 %psum.7 = s32[1024]{0:T(1024)S(1)} all-reduce(s32[1024]{0:T(1024)S(1)} %bitcast.52), channel_id=1, replica_groups=mesh['x'=4,'z'=16,'mp'=8] {'x'}, use_global_device_ids=true, to_apply=%region_1.0 | all-reduce | flops 1024 | bytes 8192 | tf_op jit(solution)/shard_map/token_ids/psum | solution.py:246
  37.1 0.0 copy-done.10
  37.1 1.6 fusion.6
  38.7 0.1 pad_maximum_fusion
  38.8 14.8 %all_to_all.40 = bf16[4,264,512]{2,1,0:T(8,128)(2,1)S(1)} all-to-all(bf16[4,264,512]{2,1,0:T(8,128)(2,1)S(1)} %pad_maximum_fusion), channel_id=1, replica_groups=mesh['x'=4,'z'=16,'mp'=8] {'x'}, dimensions={0} | all-to-all | bytes 2162688 | tf_op jit(solution)/shard_map/embedded/all_to_all | solution.py:26
  53.6 0.0 copy-start.3
  53.6 0.1 slice_reduce_fusion
  53.8 0.0 copy-start.4
  53.8 0.0 copy-start.5
  53.8 0.8 pad_maximum_fusion.2
  54.6 5.5 %all-to-all-start.2 = ((bf16[16,16,640]{2,1,0:T(8,128)(2,1)}), bf16[16,16,640]{2,1,0:T(8,128)(2,1)}, u32[]{:S(2)}, u32[]{:S(2)}) async-start(bf16[16,16,640]{2,1,0:T(8,128)(2,1)} %pad_maximum_fusion.2), calls=%async_computation.2 | async-start | bytes 655360 | tf_op jit(solution)/shard_map/embedded/all_to_all | solution.py:26
  60.1 0.0 copy-done.3
  60.1 0.0 copy-done.4
  60.1 0.0 copy-done.5
  60.2 0.0 copy-start.9
  60.2 0.0 copy-start.2
  60.2 3.1 %collective-permute-start.1 = (bf16[576,512]{1,0:T(8,128)(2,1)S(1)}, bf16[576,512]{1,0:T(8,128)(2,1)S(1)}, u32[]{:S(2)}, u32[]{:S(2)}) collective-permute-start(bf16[576,512]{1,0:T(8,128)(2,1)S(1)} %pad_maximum_fusion.1.w0_ref), channel_id=1, source_target_pairs={{0,384},{128,0},{256,128},{384,256},{1,385},{129,1},{257,129},{385... | collective-permute-start | bytes 1769480 | tf_op jit(solution)/shard_map/weights/ppermute | solution.py:229
  63.3 2.8 %collective-permute-start = (bf16[576,512]{1,0:T(8,128)(2,1)S(1)}, bf16[576,512]{1,0:T(8,128)(2,1)}, u32[]{:S(2)}, u32[]{:S(2)}) collective-permute-start(bf16[576,512]{1,0:T(8,128)(2,1)S(1)} %pad_maximum_fusion.1.w0_ref), channel_id=1, source_target_pairs={{0,128},{128,256},{256,384},{384,0},{1,129},{129,257},{257,385},{3... | collective-permute-start | bytes 1769480 | tf_op jit(solution)/shard_map/weights/ppermute | solution.py:229
  66.1 10.1 %all-to-all-done.2.got_ref = bf16[16,16,640]{2,1,0:T(8,128)(2,1)} async-done(((bf16[16,16,640]{2,1,0:T(8,128)(2,1)}), bf16[16,16,640]{2,1,0:T(8,128)(2,1)}, u32[]{:S(2)}, u32[]{:S(2)}) %all-to-all-start.2) | async-done | bytes 327712 | tf_op jit(solution)/shard_map/embedded/all_to_all | solution.py:26
  76.2 1.8 embedded.1
  78.0 0.0 collective-permute-done.1.w2_ref
  78.0 0.0 collective-permute-done.w1_ref
  78.0 10.7 %all-to-all-start.3 = ((bf16[16,16,512]{2,1,0:T(8,128)(2,1)}), bf16[16,16,512]{2,1,0:T(8,128)(2,1)S(1)}, u32[]{:S(2)}, u32[]{:S(2)}) async-start(bf16[16,16,512]{2,1,0:T(8,128)(2,1)} %get-tuple-element.16), calls=%async_computation.3 | async-start | bytes 524288 | tf_op jit(solution)/shard_map/embedded/all_to_all | solution.py:26
  88.7 1.7 slice.32
  90.4 0.7 slice.33
  91.1 1.9 %collective-permute-start.3 = (bf16[288,512]{1,0:T(8,128)(2,1)}, bf16[288,512]{1,0:T(8,128)(2,1)}, u32[]{:S(2)}, u32[]{:S(2)}) collective-permute-start(bf16[288,512]{1,0:T(8,128)(2,1)} %slice.33), channel_id=1, source_target_pairs={{0,384},{128,0},{256,128},{384,256},{1,385},{129,1},{257,129},{385... | collective-permute-start | bytes 884744 | tf_op jit(solution)/shard_map/embedded/ppermute | solution.py:291
  93.0 3.9 %collective-permute-start.2 = (bf16[288,512]{1,0:T(8,128)(2,1)}, bf16[288,512]{1,0:T(8,128)(2,1)}, u32[]{:S(2)}, u32[]{:S(2)}) collective-permute-start(bf16[288,512]{1,0:T(8,128)(2,1)} %slice.32), channel_id=1, source_target_pairs={{0,128},{128,256},{256,384},{384,0},{1,129},{129,257},{257,385},{3... | collective-permute-start | bytes 884744 | tf_op jit(solution)/shard_map/embedded/ppermute | solution.py:290
  97.0 1.3 and_select_fusion
  98.3 1.7 collective-permute-done.3.w4_ref
  100.1 3.1 %collective-permute-done.2.w3_ref = bf16[288,512]{1,0:T(8,128)(2,1)} collective-permute-done((bf16[288,512]{1,0:T(8,128)(2,1)}, bf16[288,512]{1,0:T(8,128)(2,1)}, u32[]{:S(2)}, u32[]{:S(2)}) %collective-permute-start.2) | collective-permute-done | bytes 294944 | tf_op jit(solution)/shard_map/embedded/ppermute | solution.py:290
  103.2 0.0 all-to-all-done.3
  103.2 2.0 %gate_up.1 = bf16[8,32,1792]{2,1,0:T(8,128)(2,1)S(1)} custom-call(bf16[256,512]{1,0:T(8,128)(2,1)S(1)} %bitcast.42, f32[1,512]{1,0:T(1,128)S(1)} %bitcast.43, f32[1,512]{1,0:T(1,128)S(1)} %bitcast.44, bf16[576,512]{1,0:T(8,128)(2,1)S(1)} %pad_maximum_fusion.1.w0_ref, bf16[576,512]{1,0:T(8,128)(2,1)} %collective-permute-done.w1_ref, ...), custom_call_target="tpu_custom_call" | custom-call | flops 402653184 | bytes 4194304 | tf_op jit(solution)/shard_map/gate_up/pallas_call | solution.py:298
  105.2 0.0 copy-start.1
  105.2 1.0 copy-done.1
  106.2 4.6 %all-to-all-start.4 = ((bf16[8,32,1792]{2,1,0:T(8,128)(2,1)}), bf16[8,32,1792]{2,1,0:T(8,128)(2,1)}, u32[]{:S(2)}, u32[]{:S(2)}) async-start(bf16[8,32,1792]{2,1,0:T(8,128)(2,1)} %copy-done.1), calls=%async_computation.4 | async-start | bytes 1835008 | tf_op jit(solution)/shard_map/gate_up/all_to_all | solution.py:26
  110.8 0.7 fusion.7
  111.6 0.1 reshape.205
  111.6 0.1 reduce_sum.69
  111.8 0.6 dynamic_slice.9
  112.3 0.7 divide_bitcast_fusion
  113.1 12.4 %all-to-all-done.4.got_ref = bf16[8,32,1792]{2,1,0:T(8,128)(2,1)} async-done(((bf16[8,32,1792]{2,1,0:T(8,128)(2,1)}), bf16[8,32,1792]{2,1,0:T(8,128)(2,1)}, u32[]{:S(2)}, u32[]{:S(2)}) %all-to-all-start.4) | async-done | bytes 917536 | tf_op jit(solution)/shard_map/gate_up/all_to_all | solution.py:26
  125.5 0.1 broadcast_in_dim.72.weight_ref
  125.5 1.5 hidden.1
  127.1 0.1 broadcast_in_dim.74
  127.1 12.8 %all_to_all.41.got_ref = bf16[8,32,1024]{2,1,0:T(8,128)(2,1)S(1)} all-to-all(bf16[8,32,1024]{2,1,0:T(8,128)(2,1)S(1)} %broadcast_in_dim.74), channel_id=1, replica_groups=mesh['x'=4,'z'=16,'mp'=8] {'mp'}, dimensions={0} | all-to-all | bytes 1048576 | tf_op jit(solution)/shard_map/hidden/all_to_all | solution.py:26
  139.9 2.2 %down.1 = (bf16[16,72,128]{2,1,0:T(8,128)(2,1)S(1)}, f32[16,1024]{1,0:T(8,128)}) custom-call(bf16[8,32,1024]{2,1,0:T(8,128)(2,1)S(1)} %all_to_all.41.got_ref, bf16[576,512]{1,0:T(8,128)(2,1)S(1)} %pad_maximum_fusion.1.w0_ref, bf16[576,512]{1,0:T(8,128)(2,1)} %collective-permute-done.w1_ref, bf16[576,512]{1,0:T(8,128)(2,1)S(1)} %collective-permute-done.1.w2_ref, ...), custom_call_target="tpu_custom_call" | custom-call | flops 201326592 | bytes 4194304 | tf_op jit(solution)/shard_map/down/pallas_call | solution.py:348
  142.2 31.0 %all_to_all.42 = bf16[16,72,128]{2,1,0:T(8,128)(2,1)S(1)} all-to-all(bf16[16,72,128]{2,1,0:T(8,128)(2,1)S(1)} %get-tuple-element.26), channel_id=1, replica_groups=mesh['x'=4,'z'=16,'mp'=8] {'z'}, dimensions={0} | all-to-all | bytes 589824 | tf_op jit(solution)/shard_map/down/all_to_all | solution.py:26
  173.1 0.1 convert_reduce_fusion.1
  173.3 0.6 broadcast_in_dim.75
  173.9 3.2 %all-to-all-start.7 = ((f32[4,8,128]{2,1,0:T(8,128)}), f32[4,8,128]{2,1,0:T(8,128)S(1)}, u32[]{:S(2)}, u32[]{:S(2)}) async-start(f32[4,8,128]{2,1,0:T(8,128)} %broadcast_in_dim.75), calls=%async_computation.7 | async-start | bytes 32768 | tf_op jit(solution)/shard_map/results/all_to_all | solution.py:26
  177.2 0.6 fusion.9
  177.8 4.7 %all-to-all-done.7 = f32[4,8,128]{2,1,0:T(8,128)S(1)} async-done(((f32[4,8,128]{2,1,0:T(8,128)}), f32[4,8,128]{2,1,0:T(8,128)S(1)}, u32[]{:S(2)}, u32[]{:S(2)}) %all-to-all-start.7) | async-done | bytes 16416 | tf_op jit(solution)/shard_map/results/all_to_all | solution.py:26
  182.5 0.1 squeeze.11
  182.6 0.6 copy.20
  (33 shorter events, 0.3 us)
Async XLA Ops:
  0.6 17.2 %copy-start = (bf16[64,128,128]{2,1,0:T(8,128)(2,1)S(1)}, bf16[64,128,128]{2,1,0:T(8,128)(2,1)}, u32[]{:S(2)}) copy-start(bf16[64,128,128]{2,1,0:T(8,128)(2,1)} %param.13) | copy-start | bytes 6291460
  2.3 25.8 %all-to-all-start = ((s32[16,8,128]{2,1,0:T(8,128)}), s32[16,8,128]{2,1,0:T(8,128)S(1)}, u32[]{:S(2)}, u32[]{:S(2)}) async-start(s32[16,8,128]{2,1,0:T(8,128)} %token_ids.1), calls=%async_computation | async-start | bytes 131072 | tf_op jit(solution)/shard_map/token_ids/all_to_all | solution.py:26
  17.8 19.3 %copy-start.10 = (bf16[1200,512]{1,0:T(8,128)(2,1)S(1)}, bf16[1200,512]{1,0:T(8,128)(2,1)}, u32[]{:S(2)}) copy-start(bf16[1200,512]{1,0:T(8,128)(2,1)} %param.18) | copy-start | bytes 3686404
  53.6 6.5 %copy-start.3 = (bf16[192,512]{1,0:T(8,128)(2,1)S(1)}, bf16[192,512]{1,0:T(8,128)(2,1)}, u32[]{:S(2)}) copy-start(bf16[192,512]{1,0:T(8,128)(2,1)} %param.22) | copy-start | bytes 589828
  53.8 6.4 %copy-start.4 = (bf16[512,192]{0,1:T(8,128)(2,1)S(1)}, bf16[512,192]{0,1:T(8,128)(2,1)}, u32[]{:S(2)}) copy-start(bf16[512,192]{0,1:T(8,128)(2,1)} %param.21) | copy-start | bytes 589828
  53.8 6.3 %copy-start.5 = (bf16[512,192]{0,1:T(8,128)(2,1)S(1)}, bf16[512,192]{0,1:T(8,128)(2,1)}, u32[]{:S(2)}) copy-start(bf16[512,192]{0,1:T(8,128)(2,1)} %param.20) | copy-start | bytes 589828
  54.6 21.6 %all-to-all-start.2 = ((bf16[16,16,640]{2,1,0:T(8,128)(2,1)}), bf16[16,16,640]{2,1,0:T(8,128)(2,1)}, u32[]{:S(2)}, u32[]{:S(2)}) async-start(bf16[16,16,640]{2,1,0:T(8,128)(2,1)} %pad_maximum_fusion.2), calls=%async_computation.2 | async-start | bytes 655360 | tf_op jit(solution)/shard_map/embedded/all_to_all | solution.py:26
  60.2 36.8 %copy-start.9 = (bf16[512]{0:T(512)(128)(2,1)S(1)}, bf16[512]{0:T(512)(128)(2,1)}, u32[]{:S(2)}) copy-start(bf16[512]{0:T(512)(128)(2,1)} %param.19) | copy-start | bytes 3076
  60.2 43.0 %copy-start.2 = (f32[512]{0:T(512)S(1)}, f32[512]{0:T(512)}, u32[]{:S(2)}) copy-start(f32[512]{0:T(512)} %param.23) | copy-start | bytes 6148
  60.2 17.7 %collective-permute-start.1 = (bf16[576,512]{1,0:T(8,128)(2,1)S(1)}, bf16[576,512]{1,0:T(8,128)(2,1)S(1)}, u32[]{:S(2)}, u32[]{:S(2)}) collective-permute-start(bf16[576,512]{1,0:T(8,128)(2,1)S(1)} %pad_maximum_fusion.1.w0_ref), channel_id=1, source_target_pairs={{0,384},{128,0},{256,128},{384,256},{1,385},{129,1},{257,129},{385... | collective-permute-start | bytes 1769480 | tf_op jit(solution)/shard_map/weights/ppermute | solution.py:229
  63.3 14.7 %collective-permute-start = (bf16[576,512]{1,0:T(8,128)(2,1)S(1)}, bf16[576,512]{1,0:T(8,128)(2,1)}, u32[]{:S(2)}, u32[]{:S(2)}) collective-permute-start(bf16[576,512]{1,0:T(8,128)(2,1)S(1)} %pad_maximum_fusion.1.w0_ref), channel_id=1, source_target_pairs={{0,128},{128,256},{256,384},{384,0},{1,129},{129,257},{257,385},{3... | collective-permute-start | bytes 1769480 | tf_op jit(solution)/shard_map/weights/ppermute | solution.py:229
  78.0 25.2 %all-to-all-start.3 = ((bf16[16,16,512]{2,1,0:T(8,128)(2,1)}), bf16[16,16,512]{2,1,0:T(8,128)(2,1)S(1)}, u32[]{:S(2)}, u32[]{:S(2)}) async-start(bf16[16,16,512]{2,1,0:T(8,128)(2,1)} %get-tuple-element.16), calls=%async_computation.3 | async-start | bytes 524288 | tf_op jit(solution)/shard_map/embedded/all_to_all | solution.py:26
  91.1 8.9 %collective-permute-start.3 = (bf16[288,512]{1,0:T(8,128)(2,1)}, bf16[288,512]{1,0:T(8,128)(2,1)}, u32[]{:S(2)}, u32[]{:S(2)}) collective-permute-start(bf16[288,512]{1,0:T(8,128)(2,1)} %slice.33), channel_id=1, source_target_pairs={{0,384},{128,0},{256,128},{384,256},{1,385},{129,1},{257,129},{385... | collective-permute-start | bytes 884744 | tf_op jit(solution)/shard_map/embedded/ppermute | solution.py:291
  93.0 10.1 %collective-permute-start.2 = (bf16[288,512]{1,0:T(8,128)(2,1)}, bf16[288,512]{1,0:T(8,128)(2,1)}, u32[]{:S(2)}, u32[]{:S(2)}) collective-permute-start(bf16[288,512]{1,0:T(8,128)(2,1)} %slice.32), channel_id=1, source_target_pairs={{0,128},{128,256},{256,384},{384,0},{1,129},{129,257},{257,385},{3... | collective-permute-start | bytes 884744 | tf_op jit(solution)/shard_map/embedded/ppermute | solution.py:290
  105.2 1.0 copy-start.1
  106.2 4.6 %copy-start.7 = (s32[2,1024]{1,0:T(2,128)S(1)}, s32[2,1024]{1,0:T(2,128)}, u32[]{:S(2)}) copy-start(s32[2,1024]{1,0:T(2,128)} %get-tuple-element.39) | copy-start | bytes 24580
  106.2 4.6 %copy-start.8 = (s32[2,1024]{1,0:T(2,128)S(1)}, s32[2,1024]{1,0:T(2,128)}, u32[]{:S(2)}) copy-start(s32[2,1024]{1,0:T(2,128)} %get-tuple-element.40) | copy-start | bytes 24580
  106.2 4.6 %copy-start.11 = (f32[2,32,128]{2,1,0:T(8,128)S(1)}, f32[2,32,128]{2,1,0:T(8,128)}, u32[]{:S(2)}) copy-start(f32[2,32,128]{2,1,0:T(8,128)} %get-tuple-element.23) | copy-start | bytes 98308
  106.2 19.3 %all-to-all-start.4 = ((bf16[8,32,1792]{2,1,0:T(8,128)(2,1)}), bf16[8,32,1792]{2,1,0:T(8,128)(2,1)}, u32[]{:S(2)}, u32[]{:S(2)}) async-start(bf16[8,32,1792]{2,1,0:T(8,128)(2,1)} %copy-done.1), calls=%async_computation.4 | async-start | bytes 1835008 | tf_op jit(solution)/shard_map/gate_up/all_to_all | solution.py:26
  139.9 37.2 %copy-start.6 = (f32[16,512]{1,0:T(8,128)S(1)}, f32[16,512]{1,0:T(8,128)}, u32[]{:S(2)}) copy-start(f32[16,512]{1,0:T(8,128)} %get-tuple-element.25) | copy-start | bytes 98308
  173.9 8.6 %all-to-all-start.7 = ((f32[4,8,128]{2,1,0:T(8,128)}), f32[4,8,128]{2,1,0:T(8,128)S(1)}, u32[]{:S(2)}, u32[]{:S(2)}) async-start(f32[4,8,128]{2,1,0:T(8,128)} %broadcast_in_dim.75), calls=%async_computation.7 | async-start | bytes 32768 | tf_op jit(solution)/shard_map/results/all_to_all | solution.py:26
